TPU v7x, 256 devices: a whole 4x4x8 slice. The times are simulated.
256 devices in a mesh: dp: 8 (over y, core), seq: 32 (over x, z).
Axes of the slice: x: 4, y: 4, z: 8, core: 2. Of those that a mesh axis runs over, the one named last changes fastest.
Arguments:
- tokens: bfloat16 [32768, 3072], P(('dp', 'seq')), parts along dimension 0, may hold values from -48 to 48
- tangent: bfloat16 [32768, 3072], P(('dp', 'seq')), parts along dimension 0, may hold values from -6 to 6
- bucket: int32 [8], P('dp'), parts along dimension 0, may hold values from 0 to 7
- mod_table: bfloat16 [8, 3, 3072], replicated, may hold values from -4 to 4
- mod_rate: bfloat16 [8, 3, 3072], replicated, may hold values from -4 to 4
- router: bfloat16 [3072, 32], replicated, may hold values from -0.109375 to 0.109375
- routes: int32 [32768, 2], P(('dp', 'seq')), parts along dimension 0, may hold values from 0 to 31, as said below
- w_in: bfloat16 [32, 3072, 768], P('seq'), may hold values from -0.109375 to 0.109375
- b_in: float32 [32, 768], P('seq'), may hold values from -3 to 3
- w_out: bfloat16 [32, 768, 3072], P('seq'), may hold values from -0.21875 to 0.21875
- b_out: float32 [32, 3072], P('seq'), may hold values from -3 to 3
Outputs:
- block_out: bfloat16 [32768, 3072], P(('dp', 'seq')), parts along dimension 0
- block_tangent: bfloat16 [32768, 3072], P(('dp', 'seq')), parts along dimension 0
There are 8 independent parts, one for each index of `dp`. A program takes and returns all parts, laid end to end along the dimension named above; an argument that names none is the same for every part. Nothing has to cross between parts.
Inputs may be any that keep to these rules, and one draw needn't show every extreme that they name: `routes`: each row names two different experts. In the rows of one device no expert is named more than 16 times, and one and the same expert is named exactly 16 times in the rows of every device.
All inputs are finite; a program needn't handle non-finite values.
Results may differ from a plain program's by a relative error of at most 0.0057.
Values may be sent and summed in bfloat16 or wider, within the bound.
A program may use at most 64 MiB of HBM per device.

v0:
```python
import jax
import jax.numpy as jnp
from jax import lax
from jax.sharding import PartitionSpec as P

norm_eps = 1e-06
gelu_scale = 0.7978845608
cubic_coef = 0.044715


def normalize(tokens, tangent):
    values = tokens.astype(jnp.float32)
    deltas = tangent.astype(jnp.float32)
    center = values - jnp.mean(values, axis=-1, keepdims=True)
    spread = jnp.mean(center * center, axis=-1, keepdims=True)
    inverse = lax.rsqrt(spread + norm_eps)
    normed = center * inverse
    normed_tan = (
        deltas
        - jnp.mean(deltas, axis=-1, keepdims=True)
        - normed * jnp.mean(normed * deltas, axis=-1, keepdims=True)
    ) * inverse
    return (normed, normed_tan)


def modulate(normed, normed_tan, main_row, tan_row):
    modded = (normed * (1.0 + main_row[1]) + main_row[0]).astype(jnp.bfloat16)
    modded_tan = (normed_tan * (1.0 + main_row[1]) + normed * tan_row[1] + tan_row[0]).astype(
        jnp.bfloat16
    )
    return (modded, modded_tan)


def route_weights(logit_gap, gap_tan):
    weight_one = jax.nn.sigmoid(logit_gap)
    weight_tan = weight_one * (1.0 - weight_one) * gap_tan
    return (weight_one, weight_tan)


def expert_rows(inputs, input_tan, w_first, bias_first, w_second, bias_second):
    hidden = jnp.dot(inputs, w_first, preferred_element_type=jnp.float32) + bias_first
    hidden_tan = jnp.dot(input_tan, w_first, preferred_element_type=jnp.float32)
    tanh_val = jnp.tanh(gelu_scale * (hidden + cubic_coef * hidden * hidden * hidden))
    active = (0.5 * hidden * (1.0 + tanh_val)).astype(jnp.bfloat16)
    slope_val = 0.5 * (1.0 + tanh_val) + 0.5 * hidden * (1.0 - tanh_val * tanh_val) * gelu_scale * (
        1.0 + 3.0 * cubic_coef * hidden * hidden
    )
    active_tan = (slope_val * hidden_tan).astype(jnp.bfloat16)
    result = (jnp.dot(active, w_second, preferred_element_type=jnp.float32) + bias_second).astype(
        jnp.bfloat16
    )
    result_tan = jnp.dot(active_tan, w_second, preferred_element_type=jnp.float32).astype(
        jnp.bfloat16
    )
    return (result, result_tan)


def finish(
    tokens,
    tangent,
    main_row,
    tan_row,
    weight_one,
    weight_tan,
    result_one,
    result_two,
    tan_one,
    tan_two,
):
    first_val = result_one.astype(jnp.float32)
    second_val = result_two.astype(jnp.float32)
    first_tan = tan_one.astype(jnp.float32)
    second_tan = tan_two.astype(jnp.float32)
    weight_col = weight_one[:, None]
    mixture = weight_col * first_val + (1.0 - weight_col) * second_val
    mixture_tan = (
        weight_col * first_tan
        + (1.0 - weight_col) * second_tan
        + weight_tan[:, None] * (first_val - second_val)
    )
    block_out = (tokens.astype(jnp.float32) + main_row[2] * mixture).astype(jnp.bfloat16)
    block_tangent = (
        tangent.astype(jnp.float32) + tan_row[2] * mixture + main_row[2] * mixture_tan
    ).astype(jnp.bfloat16)
    return (block_out, block_tangent)


def table_row(table, bucket):
    picked = jnp.arange(table.shape[0], dtype=jnp.int32) == bucket[0]
    return jnp.sum(jnp.where(picked[:, None, None], table.astype(jnp.float32), 0.0), axis=0)


def local(tokens, tangent, bucket, mod_table, mod_rate, router, routes, w_in, b_in, w_out, b_out):
    row_count, feat_width = tokens.shape
    group_size = lax.axis_size("seq")
    expert_count = router.shape[1]
    capacity = 4 * row_count // expert_count
    normed, normed_tan = normalize(tokens, tangent)
    main_row = table_row(mod_table, bucket)
    tan_row = table_row(mod_rate, bucket)
    modded, modded_tan = modulate(normed, normed_tan, main_row, tan_row)
    logits = jnp.dot(modded, router, preferred_element_type=jnp.float32)
    logit_tan = jnp.dot(modded_tan, router, preferred_element_type=jnp.float32)
    expert_ids = jnp.arange(expert_count, dtype=jnp.int32)[None, :]
    pick_one = routes[:, 0:1] == expert_ids
    pick_two = routes[:, 1:2] == expert_ids
    logit_gap = jnp.sum(jnp.where(pick_one, logits, 0.0), axis=1) - jnp.sum(
        jnp.where(pick_two, logits, 0.0), axis=1
    )
    gap_tan = jnp.sum(jnp.where(pick_one, logit_tan, 0.0), axis=1) - jnp.sum(
        jnp.where(pick_two, logit_tan, 0.0), axis=1
    )
    weight_one, weight_tan = route_weights(logit_gap, gap_tan)
    flat_ids = routes.reshape(-1)
    one_hot = (flat_ids[:, None] == expert_ids).astype(jnp.int32)
    before = jnp.cumsum(one_hot, axis=0) - one_hot
    rank_ids = jnp.sum(before * one_hot, axis=1)
    position = flat_ids * capacity + rank_ids
    owner_tok = jnp.arange(flat_ids.shape[0], dtype=jnp.int32) // 2
    source_row = (
        jnp.full((expert_count * capacity,), row_count, jnp.int32).at[position].set(owner_tok)
    )
    padded = jnp.concatenate([modded, jnp.zeros((1, feat_width), jnp.bfloat16)], axis=0)
    padded_tan = jnp.concatenate([modded_tan, jnp.zeros((1, feat_width), jnp.bfloat16)], axis=0)
    send_main = padded[source_row].reshape(group_size, capacity, feat_width)
    send_tan = padded_tan[source_row].reshape(group_size, capacity, feat_width)
    arrived = (
        lax.all_to_all(send_main, "seq", split_axis=0, concat_axis=0, tiled=True),
        lax.all_to_all(send_tan, "seq", split_axis=0, concat_axis=0, tiled=True),
    )
    shaped = arrived[0].shape
    result, result_tan = expert_rows(
        arrived[0].reshape(-1, feat_width),
        arrived[1].reshape(-1, feat_width),
        w_in[0],
        b_in[0],
        w_out[0],
        b_out[0],
    )
    back_pair = (
        lax.all_to_all(result.reshape(shaped), "seq", split_axis=0, concat_axis=0, tiled=True),
        lax.all_to_all(result_tan.reshape(shaped), "seq", split_axis=0, concat_axis=0, tiled=True),
    )
    back_main = back_pair[0].reshape(-1, feat_width)[position].reshape(row_count, 2, feat_width)
    back_tan = back_pair[1].reshape(-1, feat_width)[position].reshape(row_count, 2, feat_width)
    return finish(
        tokens,
        tangent,
        main_row,
        tan_row,
        weight_one,
        weight_tan,
        back_main[:, 0],
        back_main[:, 1],
        back_tan[:, 0],
        back_tan[:, 1],
    )


def solution(mesh):
    in_specs = (
        P(("dp", "seq"), None),
        P(("dp", "seq"), None),
        P("dp"),
        P(),
        P(),
        P(),
        P(("dp", "seq"), None),
        P("seq", None, None),
        P("seq", None),
        P("seq", None, None),
        P("seq", None),
    )
    out_specs = (P(("dp", "seq"), None), P(("dp", "seq"), None))
    return jax.shard_map(local, mesh=mesh, in_specs=in_specs, out_specs=out_specs, check_vma=False)
```

profile of v0, /device:TPU:1, one launch (start us, length us, event | category | flops | bytes accessed | tf_op | source)
XLA Modules:
  0.0 365.8 jit_solution(9559695991468373280)
XLA Ops:
  0.6 0.0 copy-start
  0.6 0.0 copy-start.2
  0.7 0.0 copy-start.4
  0.7 0.8 broadcast_multiply_fusion
  1.5 0.8 copy.14
  2.3 0.1 eq.77
  2.4 0.1 eq.81
  3.3 1.3 convert_reduce_fusion.1
  4.6 1.5 fusion.26
  6.1 0.1 copy.13
  6.2 0.1 mul.209
  6.4 0.6 reduce-window.6
  7.0 0.2 slice_reduce_fusion
  7.2 0.1 fusion.61
  7.3 1.4 scatter_custom_fusion
  8.7 0.3 select_reduce_fusion
  9.0 0.1 fusion.76
  9.1 0.6 convert_reduce_fusion
  9.7 1.0 fusion.25
  10.7 0.0 copy-start.6
  10.7 0.0 copy-start.7
  10.7 0.9 copy-done.6
  11.6 0.1 concatenate.6
  11.6 3.9 %gather_fusion = bf16[512,3072]{1,0:T(8,128)(2,1)} fusion(bf16[129,3072]{1,0:T(8,128)(2,1)S(1)} %concatenate.6, s32[1024]{0:T(1024)S(1)} %pad_clamp_fusion.1), kind=kCustom, calls=%fused_computation | custom fusion | bytes 6293504 | tf_op jit(solution)/shard_map/gather | solution.py:125
  15.5 12.0 %all-to-all-start = ((bf16[32,16,3072]{2,1,0:T(8,128)(2,1)}), bf16[32,16,3072]{2,1,0:T(8,128)(2,1)}, u32[]{:S(2)}, u32[]{:S(2)}) async-start(bf16[32,16,3072]{2,1,0:T(8,128)(2,1)} %bitcast.95), calls=%async_computation | async-start | bytes 6291456 | tf_op jit(solution)/shard_map/all_to_all | solution.py:128
  27.5 0.1 concatenate.7
  27.6 3.9 %gather_fusion.2 = bf16[512,3072]{1,0:T(8,128)(2,1)} fusion(bf16[129,3072]{1,0:T(8,128)(2,1)S(1)} %concatenate.7, s32[1024]{0:T(1024)S(1)} %pad_clamp_fusion.1), kind=kCustom, calls=%fused_computation.2 | custom fusion | bytes 6293504 | tf_op jit(solution)/shard_map/gather | solution.py:126
  31.5 67.6 %all-to-all-done = bf16[32,16,3072]{2,1,0:T(8,128)(2,1)} async-done(((bf16[32,16,3072]{2,1,0:T(8,128)(2,1)}), bf16[32,16,3072]{2,1,0:T(8,128)(2,1)}, u32[]{:S(2)}, u32[]{:S(2)}) %all-to-all-start) | async-done | bytes 3145760 | tf_op jit(solution)/shard_map/all_to_all | solution.py:128
  99.0 9.1 %all-to-all-start.2 = ((bf16[32,16,3072]{2,1,0:T(8,128)(2,1)}), bf16[32,16,3072]{2,1,0:T(8,128)(2,1)S(1)}, u32[]{:S(2)}, u32[]{:S(2)}) async-start(bf16[32,16,3072]{2,1,0:T(8,128)(2,1)} %bitcast.94), calls=%async_computation.2 | async-start | bytes 6291456 | tf_op jit(solution)/shard_map/all_to_all | solution.py:129
  108.2 7.0 %fusion.45 = f32[512,768]{1,0:T(8,128)} fusion(bf16[512,3072]{1,0:T(8,128)(2,1)} %bitcast.10, bf16[1,3072,768]{2,1,0:T(8,128)(2,1)} %param.18, f32[768]{0:T(1024)S(1)} %reduce.1), kind=kOutput, calls=%fused_computation.60 | convolution fusion | flops 2416312320 | bytes 9440256 | tf_op jit(solution)/shard_map/dot_general | solution.py:41
  115.2 63.8 %all-to-all-done.2 = bf16[32,16,3072]{2,1,0:T(8,128)(2,1)S(1)} async-done(((bf16[32,16,3072]{2,1,0:T(8,128)(2,1)}), bf16[32,16,3072]{2,1,0:T(8,128)(2,1)S(1)}, u32[]{:S(2)}, u32[]{:S(2)}) %all-to-all-start.2) | async-done | bytes 3145760 | tf_op jit(solution)/shard_map/all_to_all | solution.py:129
  179.0 12.8 %fusion.8 = bf16[512,3072]{1,0:T(8,128)(2,1)} fusion(bf16[1,768,3072]{2,1,0:T(8,128)(2,1)} %param.20, f32[512,768]{1,0:T(8,128)} %fusion.45, bf16[512,3072]{1,0:T(8,128)(2,1)S(1)} %bitcast.97, bf16[1,3072,768]{2,1,0:T(8,128)(2,1)} %param.18), kind=kOutput, calls=%fused_computation.14 | convolution fusion | flops 4840882176 | bytes 17301504 | tf_op jit(solution)/shard_map/dot_general | solution.py:52
  191.8 9.3 %all-to-all-start.3 = ((bf16[32,16,3072]{2,1,0:T(8,128)(2,1)}), bf16[32,16,3072]{2,1,0:T(8,128)(2,1)S(1)}, u32[]{:S(2)}, u32[]{:S(2)}) async-start(bf16[32,16,3072]{2,1,0:T(8,128)(2,1)} %bitcast.98), calls=%async_computation.3 | async-start | bytes 6291456 | tf_op jit(solution)/shard_map/all_to_all | solution.py:142
  201.2 7.2 %add_convert_fusion = bf16[512,3072]{1,0:T(8,128)(2,1)} fusion(bf16[1,768,3072]{2,1,0:T(8,128)(2,1)} %param.20, f32[3072]{0:T(1024)S(1)} %bitcast.108, f32[512,768]{1,0:T(8,128)} %fusion.45), kind=kOutput, calls=%fused_computation.5 | convolution fusion | flops 2422603776 | bytes 9449472 | tf_op jit(solution)/shard_map/dot_general | solution.py:49
  208.4 63.7 %all-to-all-done.3 = bf16[32,16,3072]{2,1,0:T(8,128)(2,1)S(1)} async-done(((bf16[32,16,3072]{2,1,0:T(8,128)(2,1)}), bf16[32,16,3072]{2,1,0:T(8,128)(2,1)S(1)}, u32[]{:S(2)}, u32[]{:S(2)}) %all-to-all-start.3) | async-done | bytes 3145760 | tf_op jit(solution)/shard_map/all_to_all | solution.py:142
  272.2 1.7 copy-done.1
  273.9 9.1 %all-to-all-start.1 = ((bf16[32,16,3072]{2,1,0:T(8,128)(2,1)}), bf16[32,16,3072]{2,1,0:T(8,128)(2,1)S(1)}, u32[]{:S(2)}, u32[]{:S(2)}) async-start(bf16[32,16,3072]{2,1,0:T(8,128)(2,1)} %bitcast.96), calls=%async_computation.1 | async-start | bytes 6291456 | tf_op jit(solution)/shard_map/all_to_all | solution.py:141
  283.0 1.5 fusion.78
  284.5 1.5 select_reduce_fusion.4
  286.0 6.7 %gather_fusion.3 = bf16[256,3072]{1,0:T(8,128)(2,1)} fusion(bf16[512,3072]{1,0:T(8,128)(2,1)} %bitcast.93, s32[1024]{0:T(1024)S(1)} %pad_clamp_fusion), kind=kCustom, calls=%fused_computation.3 | custom fusion | bytes 3146752 | tf_op jit(solution)/shard_map/gather | solution.py:145
  292.7 4.5 %reshape.148 = bf16[128,2,3072]{2,1,0:T(2,128)(2,1)} reshape(bf16[256,3072]{1,0:T(8,128)(2,1)} %gather_fusion.3) | data formatting | bytes 3145728 | tf_op jit(solution)/shard_map/reshape | solution.py:145
  297.2 5.8 %fusion.74 = (bf16[128,1,3072]{2,1,0:T(2,128)(2,1)}, bf16[128,1,3072]{2,1,0:T(2,128)(2,1)}) fusion(bf16[128,2,3072]{2,1,0:T(2,128)(2,1)} %reshape.148), kind=kLoop, calls=%fused_computation.122 | loop fusion | bytes 3145728 | tf_op jit(solution)/shard_map/slice | solution.py:155
  303.0 51.0 %all-to-all-done.1 = bf16[32,16,3072]{2,1,0:T(8,128)(2,1)S(1)} async-done(((bf16[32,16,3072]{2,1,0:T(8,128)(2,1)}), bf16[32,16,3072]{2,1,0:T(8,128)(2,1)S(1)}, u32[]{:S(2)}, u32[]{:S(2)}) %all-to-all-start.1) | async-done | bytes 3145760 | tf_op jit(solution)/shard_map/all_to_all | solution.py:141
  354.0 2.7 gather_fusion.1
  356.7 3.5 reshape.143
  360.2 2.2 fusion.75
  362.5 0.1 copy-done.9
  362.6 3.2 fusion.32
  (38 shorter events, 0.2 us)
Async XLA Ops:
  0.6 282.3 %copy-start = (bf16[3072,32]{0,1:T(8,128)(2,1)S(1)}, bf16[3072,32]{0,1:T(8,128)(2,1)}, u32[]{:S(2)}) copy-start(bf16[3072,32]{0,1:T(8,128)(2,1)} %param.16) | copy-start | bytes 589828
  0.6 8.4 %copy-start.2 = (bf16[128,3072]{1,0:T(8,128)(2,1)S(1)}, bf16[128,3072]{1,0:T(8,128)(2,1)}, u32[]{:S(2)}) copy-start(bf16[128,3072]{1,0:T(8,128)(2,1)} %param.11) | copy-start | bytes 2359300
  0.7 8.1 %copy-start.10 = (bf16[8,3,3072]{2,0,1:T(8,128)(2,1)S(1)}, bf16[8,3,3072]{2,0,1:T(8,128)(2,1)}, u32[]{:S(2)}) copy-start(bf16[8,3,3072]{2,0,1:T(8,128)(2,1)} %param.15) | copy-start | bytes 442372
  0.7 8.1 %copy-start.11 = (bf16[8,3,3072]{2,0,1:T(8,128)(2,1)S(1)}, bf16[8,3,3072]{2,0,1:T(8,128)(2,1)}, u32[]{:S(2)}) copy-start(bf16[8,3,3072]{2,0,1:T(8,128)(2,1)} %param.14) | copy-start | bytes 442372
  0.7 8.4 %copy-start.4 = (bf16[128,3072]{1,0:T(8,128)(2,1)S(1)}, bf16[128,3072]{1,0:T(8,128)(2,1)}, u32[]{:S(2)}) copy-start(bf16[128,3072]{1,0:T(8,128)(2,1)} %param.12) | copy-start | bytes 2359300
  10.7 0.9 copy-start.6
  10.7 16.8 %copy-start.7 = (bf16[128,3072]{1,0:T(8,128)(2,1)}, bf16[128,3072]{1,0:T(8,128)(2,1)S(1)}, u32[]{:S(2)}) copy-start(bf16[128,3072]{1,0:T(8,128)(2,1)S(1)} %get-tuple-element.20) | copy-start | bytes 2359300
  15.5 83.5 %all-to-all-start = ((bf16[32,16,3072]{2,1,0:T(8,128)(2,1)}), bf16[32,16,3072]{2,1,0:T(8,128)(2,1)}, u32[]{:S(2)}, u32[]{:S(2)}) async-start(bf16[32,16,3072]{2,1,0:T(8,128)(2,1)} %bitcast.95), calls=%async_computation | async-start | bytes 6291456 | tf_op jit(solution)/shard_map/all_to_all | solution.py:128
  99.0 9.1 %copy-start.13 = (f32[1,768]{1,0:T(1,128)S(1)}, f32[1,768]{1,0:T(1,128)}, u32[]{:S(2)}) copy-start(f32[1,768]{1,0:T(1,128)} %param.19) | copy-start | bytes 9220
  99.0 80.0 %all-to-all-start.2 = ((bf16[32,16,3072]{2,1,0:T(8,128)(2,1)}), bf16[32,16,3072]{2,1,0:T(8,128)(2,1)S(1)}, u32[]{:S(2)}, u32[]{:S(2)}) async-start(bf16[32,16,3072]{2,1,0:T(8,128)(2,1)} %bitcast.94), calls=%async_computation.2 | async-start | bytes 6291456 | tf_op jit(solution)/shard_map/all_to_all | solution.py:129
  191.8 9.4 %copy-start.14 = (f32[1,3072]{1,0:T(1,128)S(1)}, f32[1,3072]{1,0:T(1,128)}, u32[]{:S(2)}) copy-start(f32[1,3072]{1,0:T(1,128)} %param.21) | copy-start | bytes 36868
  191.8 80.3 %all-to-all-start.3 = ((bf16[32,16,3072]{2,1,0:T(8,128)(2,1)}), bf16[32,16,3072]{2,1,0:T(8,128)(2,1)S(1)}, u32[]{:S(2)}, u32[]{:S(2)}) async-start(bf16[32,16,3072]{2,1,0:T(8,128)(2,1)} %bitcast.98), calls=%async_computation.3 | async-start | bytes 6291456 | tf_op jit(solution)/shard_map/all_to_all | solution.py:142
  272.2 1.7 copy-start.1
  272.2 10.8 %copy-start.12 = (s32[128,2]{0,1:T(2,128)S(1)}, s32[128,2]{0,1:T(2,128)}, u32[]{:S(2)}) copy-start(s32[128,2]{0,1:T(2,128)} %param.17) | copy-start | bytes 3076
  273.9 80.1 %all-to-all-start.1 = ((bf16[32,16,3072]{2,1,0:T(8,128)(2,1)}), bf16[32,16,3072]{2,1,0:T(8,128)(2,1)S(1)}, u32[]{:S(2)}, u32[]{:S(2)}) async-start(bf16[32,16,3072]{2,1,0:T(8,128)(2,1)} %bitcast.96), calls=%async_computation.1 | async-start | bytes 6291456 | tf_op jit(solution)/shard_map/all_to_all | solution.py:141
  360.2 2.3 copy-start.3
  360.2 2.3 copy-start.5
  360.2 2.3 copy-start.8
  360.2 2.3 copy-start.9
where the time goes:
time: 369 us; the launch traced here: 366 us
  waiting for transfers between devices  246 us (67%)
  starting transfers between devices  39.5 us (11%)
  local copies, waits for them, and re-layouts  38.9 us (11%)
  matrix products  30.1 us (8%)
  other arithmetic  9.55 us (3%)
    all_to_all x1, waiting for transfers between devices, local(): lax.all_to_all(send_main, 'seq', split_axis=0, concat_axis=0, tiled=True)  67.6 us
    all_to_all x1, waiting for transfers between devices, local(): lax.all_to_all(send_tan, 'seq', split_axis=0, concat_axis=0, tiled=True)  63.8 us
    all_to_all x1, waiting for transfers between devices, local(): lax.all_to_all(result_tan.reshape(shaped), 'seq', split_axis=0, concat_ax...  63.7 us
    all_to_all x1, waiting for transfers between devices, local(): lax.all_to_all(result.reshape(shaped), 'seq', split_axis=0, concat_axis=0...  51 us
    dot_general x1, matrix products, expert_rows(): jnp.dot(active_tan, w_second, preferred_element_type=jnp.float32)  12.8 us
    all_to_all x1, starting transfers between devices, local(): lax.all_to_all(send_main, 'seq', split_axis=0, concat_axis=0, tiled=True)  12 us
    all_to_all x1, starting transfers between devices, local(): lax.all_to_all(result_tan.reshape(shaped), 'seq', split_axis=0, concat_ax...  9.34 us
    all_to_all x1, starting transfers between devices, local(): lax.all_to_all(send_tan, 'seq', split_axis=0, concat_axis=0, tiled=True)  9.12 us
  transfers between devices with their start and end apart: 4, of which 4 were waited for; matrix products, arithmetic and copies ran while one was open for 10% of the time, Pallas kernels for 0%

commit v1 on v0

v1 whole, which is shorter than its diff:
```python
import functools

import jax
import jax.numpy as jnp
from jax import lax
from jax.experimental import pallas as pl
from jax.experimental.pallas import tpu as pltpu
from jax.sharding import PartitionSpec as P

norm_eps = 1e-06
gelu_scale = 0.7978845608
cubic_coef = 0.044715

MESH = pl.DeviceIdType.MESH
F32 = jnp.float32
BF16 = jnp.bfloat16

X, Y, Z = 4, 4, 8
GROUPS = 4
BLOCKS = 8
SLOTS = GROUPS * BLOCKS
SEND_ORDER = (3, 1, 2, 0)
CHUNKS = 2


def kernel(
    tok, tan, bucket, table, rate, router, routes, routes_t, w_in, b_in, w_out, b_out,
    out, out_tan,
    modded, modded_tan, tx, rx, back, acc, mix_hi, mix_lo, hid, wbi, wbo, sgi, sgo, bbi, bbo,
    send_sem, recv_sem, ret_send, ret_recv, w_sem, stage_send, stage_recv, fwd_send, bias_send, bias_recv,
):
    rows, width = tok.shape
    cap = tx.shape[1] // 2
    hidden_width = wbi.shape[1]
    dp, seq = lax.axis_index("dp"), lax.axis_index("seq")
    y, core = dp // 2, dp % 2
    x, z = seq // Z, seq % Z
    two = 2 - 4 * (z % 2)
    shift = (0, 1, -1, two)
    span = BLOCKS * 2 * cap

    def device(dy, c, dx, dz):
        return {
            "dp": ((y + dy) % Y) * 2 + c,
            "seq": ((x + dx) % X) * Z + (z + dz + Z) % Z,
        }

    barrier = pltpu.get_barrier_semaphore()
    peers = [
        device(0, (core + dc) % 2, dx, dz)
        for dz in (0, 1, -1, 2, -2) for dx in range(X) for dc in range(2)
        if (dz, dx, dc) != (0, 0, 0)
    ]
    peers += [device(0, core, 0, 4)]
    peers += [device(dy, c, 0, 0) for dy in range(1, Y) for c in range(2)]
    for peer in peers:
        pl.semaphore_signal(barrier, inc=1, device_id=peer, device_id_type=MESH)
    pl.semaphore_wait(barrier, len(peers))

    part_in, part_out = sgi.shape[0], sgo.shape[0]
    step_in, step_out = part_in // CHUNKS, part_out // CHUNKS
    half = device(0, core, 0, 4)
    stages = []
    for k in range(CHUNKS):
        stages.append(pltpu.make_async_remote_copy(
            w_in.at[0, pl.ds(dp * part_in + k * step_in, step_in)], sgi.at[pl.ds(k * step_in, step_in)],
            stage_send.at[k], stage_recv.at[k], device_id=half, device_id_type=MESH))
    for k in range(CHUNKS):
        stages.append(pltpu.make_async_remote_copy(
            w_out.at[0, pl.ds(dp * part_out + k * step_out, step_out)], sgo.at[pl.ds(k * step_out, step_out)],
            stage_send.at[CHUNKS + k], stage_recv.at[CHUNKS + k], device_id=half, device_id_type=MESH))
    biases = [
        pltpu.make_async_remote_copy(b_in, bbi, bias_send.at[0], bias_recv.at[0], device_id=half, device_id_type=MESH),
        pltpu.make_async_remote_copy(b_out, bbo, bias_send.at[1], bias_recv.at[1], device_id=half, device_id_type=MESH),
    ]
    for copy in biases + stages:
        copy.start()

    @pl.when(core == 0)
    def _():
        pltpu.make_async_copy(w_in.at[0], wbi, w_sem.at[0]).start()
        pltpu.make_async_copy(w_out.at[0], wbo, w_sem.at[1]).start()

    row = bucket[0]
    main_row = table[row].astype(F32)
    tan_row = rate[row].astype(F32)
    scale = 1.0 + main_row[1:2]
    offset = main_row[0:1]
    scale_tan = tan_row[1:2]
    offset_tan = tan_row[0:1]

    @pl.loop(0, rows // 16)
    def _(i):
        at = pl.ds(pl.multiple_of(i * 16, 16), 16)
        values = tok[at].astype(F32)
        deltas = tan[at].astype(F32)
        center = values - jnp.mean(values, axis=-1, keepdims=True)
        spread = jnp.mean(center * center, axis=-1, keepdims=True)
        inverse = lax.rsqrt(spread + norm_eps)
        normed = center * inverse
        normed_tan = (
            deltas
            - jnp.mean(deltas, axis=-1, keepdims=True)
            - normed * jnp.mean(normed * deltas, axis=-1, keepdims=True)
        ) * inverse
        modded[at] = (normed * scale + offset).astype(BF16)
        modded_tan[at] = (normed_tan * scale + normed * scale_tan + offset_tan).astype(BF16)

    one_t, two_t = routes_t[0:1], routes_t[1:2]
    early = (
        lax.broadcasted_iota(jnp.int32, (rows, rows), 0) < lax.broadcasted_iota(jnp.int32, (rows, rows), 1)
    ).astype(BF16)
    line = lax.broadcasted_iota(jnp.int32, (BLOCKS * cap, rows), 0)
    for g in SEND_ORDER:
        block = line // cap
        expert = (block // 2) * Z + (z + shift[g] + 4 * (block % 2) + Z) % Z
        named = (one_t == expert) | (two_t == expert)
        rank = jnp.dot(named.astype(F32).astype(BF16), early, preferred_element_type=F32)
        pick = (named & (rank == (line % cap).astype(F32))).astype(F32).astype(BF16)

        @pl.loop(0, width // 512)
        def _(n, g=g, pick=pick):
            cols = pl.ds(pl.multiple_of(n * 512, 512), 512)
            for source, first in ((modded, 0), (modded_tan, cap)):
                packed = jnp.dot(pick, source[:, cols], preferred_element_type=F32).astype(BF16)
                tx[pl.ds(g * BLOCKS, BLOCKS), pl.ds(first, cap), cols] = packed.reshape(BLOCKS, cap, 512)

        for dx in range(X):
            to_x = (x + dx) % X
            for c in range(2):
                to_core = (core + c) % 2
                slot = g * BLOCKS + to_x * 2 + to_core
                mine = g * BLOCKS + x * 2 + core
                if (g, dx, c) == (0, 0, 0):
                    pltpu.make_async_copy(tx.at[slot], rx.at[mine], recv_sem.at[g]).start()
                else:
                    pltpu.make_async_remote_copy(
                        tx.at[slot], rx.at[mine], send_sem.at[0], recv_sem.at[g],
                        device_id=device(0, to_core, dx, shift[g]), device_id_type=MESH,
                    ).start()

    logits = jnp.dot(modded[...], router[...], preferred_element_type=F32)
    logit_tan = jnp.dot(modded_tan[...], router[...], preferred_element_type=F32)
    one, second = routes[:, 0:1], routes[:, 1:2]
    lane = lax.broadcasted_iota(jnp.int32, logits.shape, 1)

    def gap(values):
        return jnp.sum(jnp.where(lane == one, values, 0.0), axis=1, keepdims=True) - jnp.sum(
            jnp.where(lane == second, values, 0.0), axis=1, keepdims=True)

    weight = 1.0 / (1.0 + jnp.exp(-gap(logits)))
    weight_tan = weight * (1.0 - weight) * gap(logit_tan)
    late = (
        lax.broadcasted_iota(jnp.int32, (rows, rows), 1) < lax.broadcasted_iota(jnp.int32, (rows, rows), 0)
    ).astype(BF16)
    spot = lax.broadcasted_iota(jnp.int32, (rows, span), 1)
    for g in range(GROUPS):
        block = spot // (2 * cap)
        expert = (block // 2) * Z + (z + shift[g] + 4 * (block % 2) + Z) % Z
        is_one, is_two = one == expert, second == expert
        named = is_one | is_two
        rank = jnp.dot(late, named.astype(F32).astype(BF16), preferred_element_type=F32)
        chosen = named & (rank == (spot % cap).astype(F32))
        is_main = (spot % (2 * cap)) < cap
        share = jnp.where(is_one, weight, 1.0 - weight)
        share_tan = jnp.where(is_one, weight_tan, -weight_tan)
        for first, value in (
            (0, jnp.where(chosen & is_main, share, 0.0)),
            (rows, jnp.where(chosen, jnp.where(is_main, share_tan, share), 0.0)),
        ):
            high = value.astype(BF16)
            mix_hi[g, pl.ds(first, rows)] = high
            mix_lo[g, pl.ds(first, rows)] = (value - high.astype(F32)).astype(BF16)

    for k in range(2 * CHUNKS):
        stages[k].wait_recv()
        if k < CHUNKS:
            src = sgi.at[pl.ds(k * step_in, step_in)]
            dst = wbi.at[pl.ds(dp * part_in + k * step_in, step_in)]
            sem = w_sem.at[0]
        else:
            src = sgo.at[pl.ds((k - CHUNKS) * step_out, step_out)]
            dst = wbo.at[pl.ds(dp * part_out + (k - CHUNKS) * step_out, step_out)]
            sem = w_sem.at[1]
        for dy in range(1, Y):
            pltpu.make_async_remote_copy(
                src, dst, fwd_send.at[k], sem, device_id=device(dy, 1, 0, 0), device_id_type=MESH).start()

        @pl.when(core == 0)
        def _(src=src, dst=dst, sem=sem, k=k):
            pltpu.make_async_remote_copy(
                src, dst, fwd_send.at[k], sem, device_id=device(0, 1, 0, 0), device_id_type=MESH).start()

        @pl.when(core == 1)
        def _(src=src, dst=dst, sem=sem):
            pltpu.make_async_copy(src, dst, sem).start()

    for copy in biases:
        copy.wait()
    bias_in = jnp.where(core == 0, b_in[...], bbi[...])
    bias_out = jnp.where(core == 0, b_out[...], bbo[...])
    acc[pl.ds(0, 1), :] = bias_out
    acc[pl.ds(8, 1), pl.ds(0, hidden_width)] = bias_in

    for g in range(GROUPS):
        held = pl.ds(g * BLOCKS, BLOCKS)
        pltpu.make_async_copy(rx.at[held], rx.at[held], recv_sem.at[g]).wait()
        if g == 0:
            pltpu.make_async_copy(wbi, wbi, w_sem.at[0]).wait()

        @pl.loop(0, hidden_width // 256)
        def _(n, held=held):
            cols = pl.ds(pl.multiple_of(n * 256, 256), 256)
            both = jnp.dot(
                rx[held].reshape(span, width), wbi[:, cols], preferred_element_type=F32
            ).reshape(BLOCKS, 2 * cap, 256)
            hidden = both[:, :cap] + acc[pl.ds(8, 1), cols].reshape(1, 1, 256)
            hidden_tan = both[:, cap:]
            tanh_val = jnp.tanh(gelu_scale * (hidden + cubic_coef * hidden * hidden * hidden))
            hid[:, pl.ds(0, cap), cols] = (0.5 * hidden * (1.0 + tanh_val)).astype(BF16)
            slope = 0.5 * (1.0 + tanh_val) + 0.5 * hidden * (1.0 - tanh_val * tanh_val) * gelu_scale * (
                1.0 + 3.0 * cubic_coef * hidden * hidden
            )
            hid[:, pl.ds(cap, cap), cols] = (slope * hidden_tan).astype(BF16)

        if g == 0:
            pltpu.make_async_copy(wbo, wbo, w_sem.at[1]).wait()

        @pl.loop(0, width // 512)
        def _(n, held=held):
            cols = pl.ds(pl.multiple_of(n * 512, 512), 512)
            both = jnp.dot(
                hid[...].reshape(span, hidden_width), wbo[:, cols], preferred_element_type=F32
            ).reshape(BLOCKS, 2 * cap, 512)
            rx[held, pl.ds(0, cap), cols] = (
                both[:, :cap] + acc[pl.ds(0, 1), cols].reshape(1, 1, 512)).astype(BF16)
            rx[held, pl.ds(cap, cap), cols] = both[:, cap:].astype(BF16)

        for dx in range(X):
            to_x = (x + dx) % X
            for c in range(2):
                to_core = (core + c) % 2
                slot = g * BLOCKS + to_x * 2 + to_core
                mine = g * BLOCKS + x * 2 + core
                if (g, dx, c) == (0, 0, 0):
                    pltpu.make_async_copy(rx.at[slot], back.at[mine], ret_recv.at[g]).start()
                else:
                    pltpu.make_async_remote_copy(
                        rx.at[slot], back.at[mine], ret_send.at[0], ret_recv.at[g],
                        device_id=device(0, to_core, dx, -shift[g]), device_id_type=MESH,
                    ).start()

    for g in range(GROUPS):
        held = pl.ds(g * BLOCKS, BLOCKS)
        pltpu.make_async_copy(back.at[held], back.at[held], ret_recv.at[g]).wait()

        @pl.loop(0, width // 512)
        def _(n, g=g, held=held):
            cols = pl.ds(pl.multiple_of(n * 512, 512), 512)
            parts = back[held, :, cols].reshape(span, 512)
            mixed = jnp.dot(mix_hi[g], parts, preferred_element_type=F32) + jnp.dot(
                mix_lo[g], parts, preferred_element_type=F32)
            if g > 0:
                mixed = mixed + acc[:, cols]
            if g < GROUPS - 1:
                acc[:, cols] = mixed
            else:
                gate = table[row, 2:3, cols].astype(F32)
                gate_tan = rate[row, 2:3, cols].astype(F32)
                mixture, mixture_tan = mixed[:rows], mixed[rows:]
                out[:, cols] = (tok[:, cols].astype(F32) + gate * mixture).astype(BF16)
                out_tan[:, cols] = (
                    tan[:, cols].astype(F32) + gate_tan * mixture + gate * mixture_tan).astype(BF16)

    pltpu.make_async_copy(tx.at[pl.ds(0, SLOTS - 1)], tx.at[pl.ds(0, SLOTS - 1)], send_sem.at[0]).wait()
    pltpu.make_async_copy(rx.at[pl.ds(0, SLOTS - 1)], rx.at[pl.ds(0, SLOTS - 1)], ret_send.at[0]).wait()
    for k in range(2 * CHUNKS):
        stages[k].wait_send()
        if k < CHUNKS:
            piece = sgi.at[pl.ds(0, step_in)]
            three = wbi.at[pl.ds(0, 3 * step_in)]
        else:
            piece = sgo.at[pl.ds(0, step_out)]
            three = wbo.at[pl.ds(0, 3 * step_out)]
        pltpu.make_async_copy(three, three, fwd_send.at[k]).wait()

        @pl.when(core == 0)
        def _(piece=piece, k=k):
            pltpu.make_async_copy(piece, piece, fwd_send.at[k]).wait()


def local(tokens, tangent, bucket, mod_table, mod_rate, router, routes, w_in, b_in, w_out, b_out):
    rows, width = tokens.shape
    hidden_width = w_in.shape[2]
    cap = 4 * rows // router.shape[1]
    devices = lax.axis_size("dp")
    vmem = pl.BlockSpec(memory_space=pltpu.VMEM)
    smem = pl.BlockSpec(memory_space=pltpu.SMEM)
    hbm = pl.BlockSpec(memory_space=pl.ANY)
    shape = jax.ShapeDtypeStruct((rows, width), BF16)
    dma = pltpu.SemaphoreType.DMA
    return tuple(pl.pallas_call(
        kernel,
        out_shape=(shape, shape),
        in_specs=[vmem, vmem, smem, vmem, vmem, vmem, vmem, vmem, hbm, vmem, hbm, vmem],
        out_specs=(vmem, vmem),
        scratch_shapes=[
            pltpu.VMEM((rows, width), BF16),
            pltpu.VMEM((rows, width), BF16),
            pltpu.VMEM((SLOTS, 2 * cap, width), BF16),
            pltpu.VMEM((SLOTS, 2 * cap, width), BF16),
            pltpu.VMEM((SLOTS, 2 * cap, width), BF16),
            pltpu.VMEM((2 * rows, width), F32),
            pltpu.VMEM((GROUPS, 2 * rows, BLOCKS * 2 * cap), BF16),
            pltpu.VMEM((GROUPS, 2 * rows, BLOCKS * 2 * cap), BF16),
            pltpu.VMEM((BLOCKS, 2 * cap, hidden_width), BF16),
            pltpu.VMEM((width, hidden_width), BF16),
            pltpu.VMEM((hidden_width, width), BF16),
            pltpu.VMEM((width // devices, hidden_width), BF16),
            pltpu.VMEM((hidden_width // devices, width), BF16),
            pltpu.VMEM((1, hidden_width), F32),
            pltpu.VMEM((1, width), F32),
            dma((1,)), dma((GROUPS,)), dma((1,)), dma((GROUPS,)),
            dma((2,)), dma((2 * CHUNKS,)), dma((2 * CHUNKS,)), dma((2 * CHUNKS,)), dma((2,)), dma((2,)),
        ],
        compiler_params=pltpu.CompilerParams(
            collective_id=0, has_side_effects=True, vmem_limit_bytes=56 << 20),
    )(tokens, tangent, bucket, mod_table, mod_rate, router, routes, routes.T, w_in, b_in, w_out, b_out))


def solution(mesh):
    in_specs = (
        P(("dp", "seq"), None),
        P(("dp", "seq"), None),
        P("dp"),
        P(),
        P(),
        P(),
        P(("dp", "seq"), None),
        P("seq", None, None),
        P("seq", None),
        P("seq", None, None),
        P("seq", None),
    )
    out_specs = (P(("dp", "seq"), None), P(("dp", "seq"), None))
    return jax.shard_map(local, mesh=mesh, in_specs=in_specs, out_specs=out_specs, check_vma=False)
```

time: 369 us -> 273 us (0.74)
  Pallas kernels: 0 us -> 256 us
  waiting for transfers between devices: 246 us -> 0 us
  starting transfers between devices: 39.5 us -> 0 us
  matrix products: 30.1 us -> 0 us
  local copies, waits for them, and re-layouts: 38.9 us -> 11.1 us
  other arithmetic: 9.55 us -> 0 us
    pallas_call x0 -> x1, Pallas kernels: none -> 256 us  [local(): pl.pallas_call(kernel, out_shape=(shape, shape), in_specs=[vmem, vmem, sm...]
    all_to_all x4 -> x0, waiting for transfers between devices: 246 us -> none  [the longest x1 67.6 us: local(): lax.all_to_all(send_main, 'seq', split_axis=0, concat_axis=0, tiled=True)]
    all_to_all x4 -> x0, starting transfers between devices: 39.5 us -> none  [the longest x1 12 us: local(): lax.all_to_all(send_main, 'seq', split_axis=0, concat_axis=0, tiled=True)]
    dot_general x5 -> x0, matrix products: 30.1 us -> none  [the longest x1 12.8 us: expert_rows(): jnp.dot(active_tan, w_second, preferred_element_type=jnp.float32)]
    gather x4 -> x0, local copies, waits for them, and re-layouts: 17.2 us -> none  [the longest x1 6.68 us: local(): back_pair[1].reshape(-1, feat_width)[position]]
    slice x3 -> x0, local copies, waits for them, and re-layouts: 8.22 us -> none  [the longest x1 5.8 us: local(): back_tan[:, 0]]
    reshape x2 -> x0, local copies, waits for them, and re-layouts: 7.96 us -> none  [the longest x1 4.46 us: local(): back_pair[1].reshape(-1, feat_width)[position]]
    unnamed x31 -> x6, local copies, waits for them, and re-layouts: 3.46 us -> 11.1 us
  transfers between devices with their start and end apart: 4 -> 0, of which waited for: 4 -> 0; matrix products, arithmetic and copies ran while one was open for 10% -> 0% of each run, Pallas kernels for 0% -> 0%
where the time goes in v1:
time: 273 us; the launch traced here: 269 us
  Pallas kernels  256 us (94%)
  local copies, waits for them, and re-layouts  11.1 us (4%)
    pallas_call x1, Pallas kernels, local(): pl.pallas_call(kernel, out_shape=(shape, shape), in_specs=[vmem, vmem, sm...  256 us
    unnamed x6, local copies, waits for them, and re-layouts  11.1 us

profile of v1, /device:TPU:1, one launch (start us, length us, event | category | flops | bytes accessed | tf_op | source)
XLA Modules:
  0.0 268.5 jit_solution(2327681388259582447)
XLA Ops:
  1.3 1.4 copy.16.routes
  2.7 1.7 copy.13.table
  4.4 1.7 copy.14.rate
  6.1 2.1 copy.15.router
  8.2 256.2 %shard_map.122 = (bf16[128,3072]{1,0:T(8,128)(2,1)}, bf16[128,3072]{1,0:T(8,128)(2,1)}) custom-call(bf16[128,3072]{1,0:T(8,128)(2,1)} %tok.1, bf16[128,3072]{1,0:T(8,128)(2,1)} %tan.1, s32[1]{0:T(128)S(6)} %copy.19.bucket, bf16[8,3,3072]{2,1,0:T(4,128)(2,1)} %copy.13.table, bf16[8,3,3072]{2,1,0:T(4,128)(2,1)} %copy.14.rate, bf16[3072,32]{1,0:T(8,128)(2,1)} %copy.15.router, ...), custom_call_target="tpu_custom_call" | custom-call | tf_op jit(solution)/shard_map/pallas_call | solution.py:302
  264.4 2.1 copy.20
  266.4 2.1 copy.21

commit v2 on v1

v2 whole, which is shorter than its diff:
```python
import jax
import jax.numpy as jnp
from jax import lax
from jax.experimental import pallas as pl
from jax.experimental.pallas import tpu as pltpu
from jax.sharding import PartitionSpec as P

norm_eps = 1e-06
gelu_scale = 0.7978845608
cubic_coef = 0.044715

MESH = pl.DeviceIdType.MESH
F32 = jnp.float32
BF16 = jnp.bfloat16

X, Y, Z = 4, 4, 8
BATCHES = 4
BLOCKS = 8
SLOTS = BATCHES * BLOCKS
SEND_ORDER = (2, 0, 3, 1)
WORK_ORDER = (0, 2, 3, 1)
CHUNKS = 2
UP, DOWN, FAR = 0, 1, 2
HOME = ((1, 0), (1, 1), (0, 1))


def wait_bytes(ref, sem):
    pltpu.make_async_copy(ref, ref, sem).wait()


def kernel(
    tok, tan, bucket, table, rate, router, routes_t, w_in, b_in, w_out, b_out,
    out, out_tan,
    modded, modded_tan, tx, rx, back, acc, mix_hi, mix_lo, hid, mods, wbi, wbo, near_in, near_out, far_in, far_out,
    bias_in, bias_out, bi_up, bi_down, bi_far, bo_up, bo_down, bo_far,
    send_sem, recv_sem, ret_send, ret_recv, own_sem, near_send, near_recv, far_send, far_recv,
    spread_send, rest_sem, first_sem, pass_send, bias_send, bias_recv,
):
    rows, width = tok.shape
    cap = tx.shape[1] // 2
    hidden_width = wbi.shape[2]
    dp, seq = lax.axis_index("dp"), lax.axis_index("seq")
    y, core = dp // 2, dp % 2
    x, z = seq // Z, seq % Z
    span = BLOCKS * 2 * cap

    def device(dy, c, to_x, dz):
        return {"dp": ((y + dy + Y) % Y) * 2 + c, "seq": to_x * Z + (z + dz + Z) % Z}

    def remote(src, dst, send, recv, to):
        return pltpu.make_async_remote_copy(src, dst, send, recv, device_id=to, device_id_type=MESH)

    barrier = pltpu.get_barrier_semaphore()
    peers = [
        device(0, (core + dc) % 2, (x + dx) % X, dz)
        for dz in (0, 1, -1) for dx in range(X) for dc in range(2)
        if (dz, dx, dc) != (0, 0, 0)
    ]
    peers += [device(0, core, x, dz) for dz in (2, -2, 4)]
    peers += [device(dy, c, x, 0) for dy in (1, -1) for c in range(2)]
    for peer in peers:
        pl.semaphore_signal(barrier, inc=1, device_id=peer, device_id_type=MESH)
    pl.semaphore_wait(barrier, len(peers))

    part = (near_in.shape[1], near_out.shape[1])
    step = (part[0] // CHUNKS, part[1] // CHUNKS)
    units = [(a, k) for a in range(2) for k in range(CHUNKS)]
    near, far, full, held = (near_in, near_out), (far_in, far_out), (w_in, w_out), (wbi, wbo)

    def near_copy(a, k, kind):
        return remote(
            full[a].at[0, pl.ds(dp * part[a] + k * step[a], step[a])],
            near[a].at[kind, pl.ds(k * step[a], step[a])],
            near_send.at[a], near_recv.at[kind, a * CHUNKS + k],
            device(0, core, x, -2 if kind == UP else 2))

    def far_copy(a, k):
        kind = DOWN if a == 0 else UP
        return remote(
            near[a].at[kind, pl.ds(k * step[a], step[a])], far[a].at[pl.ds(k * step[a], step[a])],
            far_send.at[a], far_recv.at[a * CHUNKS + k],
            device(0, core, x, 2 if kind == DOWN else -2))

    biases = []
    for kind, dz, to_in, to_out in ((UP, -2, bi_up, bo_up), (DOWN, 2, bi_down, bo_down), (FAR, 4, bi_far, bo_far)):
        to = device(0, core, x, dz)
        biases.append(remote(b_in, to_in, bias_send.at[0, kind], bias_recv.at[0, kind], to))
        biases.append(remote(b_out, to_out, bias_send.at[1, kind], bias_recv.at[1, kind], to))
    for a, k in units:
        for kind in (UP, DOWN):
            near_copy(a, k, kind).start()
    for copy in biases:
        copy.start()

    @pl.when(core == 0)
    def _():
        pltpu.make_async_copy(w_in.at[0], wbi.at[0], own_sem.at[0]).start()
        pltpu.make_async_copy(w_out.at[0], wbo.at[0], own_sem.at[1]).start()

    at_row = lax.broadcasted_iota(jnp.int32, (table.shape[1], width), 0) == bucket[0]
    for k in range(3):
        for first, source in ((0, table), (3, rate)):
            mods[pl.ds(first + k, 1)] = jnp.sum(
                jnp.where(at_row, source[k].astype(F32), 0.0), axis=0, keepdims=True)
    offset, offset_tan = mods[pl.ds(0, 1)], mods[pl.ds(3, 1)]
    scale, scale_tan = 1.0 + mods[pl.ds(1, 1)], mods[pl.ds(4, 1)]

    @pl.loop(0, rows // 16)
    def _(i):
        at = pl.ds(pl.multiple_of(i * 16, 16), 16)
        values = tok[at].astype(F32)
        deltas = tan[at].astype(F32)
        center = values - jnp.mean(values, axis=-1, keepdims=True)
        spread = jnp.mean(center * center, axis=-1, keepdims=True)
        inverse = lax.rsqrt(spread + norm_eps)
        normed = center * inverse
        normed_tan = (
            deltas
            - jnp.mean(deltas, axis=-1, keepdims=True)
            - normed * jnp.mean(normed * deltas, axis=-1, keepdims=True)
        ) * inverse
        modded[at] = (normed * scale + offset).astype(BF16)
        modded_tan[at] = (normed_tan * scale + normed * scale_tan + offset_tan).astype(BF16)

    def expert_of(block, batch):
        group, place = batch // 2, batch % 2
        to_x, to_core = block // 2, block % 2
        return to_x * Z + (z + group * (1 - 2 * ((x + to_x) % 2)) + to_core * 2 + place * 4 + Z) % Z

    one_t, two_t = routes_t[0:1], routes_t[1:2]
    square = (rows, rows)
    down, across = lax.broadcasted_iota(jnp.int32, square, 0), lax.broadcasted_iota(jnp.int32, square, 1)
    early = (down < across).astype(F32).astype(BF16)
    late = (across < down).astype(F32).astype(BF16)
    line = lax.broadcasted_iota(jnp.int32, (BLOCKS * cap, rows), 0)
    mine = x * 2 + core
    for batch in SEND_ORDER:
        expert = expert_of(line // cap, batch)
        named = (one_t == expert) | (two_t == expert)
        rank = jnp.dot(named.astype(F32).astype(BF16), early, preferred_element_type=F32)
        pick = (named & (rank == (line % cap).astype(F32))).astype(F32).astype(BF16)

        @pl.loop(0, width // 512)
        def _(n, batch=batch, pick=pick):
            cols = pl.ds(pl.multiple_of(n * 512, 512), 512)
            for source, first in ((modded, 0), (modded_tan, cap)):
                packed = jnp.dot(pick, source[:, cols], preferred_element_type=F32).astype(BF16)
                tx[pl.ds(batch * BLOCKS, BLOCKS), pl.ds(first, cap), cols] = packed.reshape(BLOCKS, cap, 512)

        for dx in range(X):
            to_x = (x + dx) % X
            dz = (batch // 2) * (1 - 2 * (dx % 2))
            for c in range(2):
                to_core = (core + c) % 2
                src = tx.at[batch * BLOCKS + to_x * 2 + to_core]
                dst = rx.at[batch * BLOCKS + mine]
                if (dx, dz, c) == (0, 0, 0):
                    pltpu.make_async_copy(src, dst, recv_sem.at[batch]).start()
                else:
                    remote(src, dst, send_sem.at[0], recv_sem.at[batch], device(0, to_core, to_x, dz)).start()

    turn = (((1,), (1,)), ((), ()))
    logits = lax.dot_general(modded[...], router[...], turn, preferred_element_type=F32)
    logit_tan = lax.dot_general(modded_tan[...], router[...], turn, preferred_element_type=F32)
    one = jnp.sum(jnp.where(down == across, one_t, 0).astype(F32), axis=1, keepdims=True).astype(jnp.int32)
    second = jnp.sum(jnp.where(down == across, two_t, 0).astype(F32), axis=1, keepdims=True).astype(jnp.int32)
    lane = lax.broadcasted_iota(jnp.int32, logits.shape, 1)

    def gap(values):
        return jnp.sum(jnp.where(lane == one, values, 0.0), axis=1, keepdims=True) - jnp.sum(
            jnp.where(lane == second, values, 0.0), axis=1, keepdims=True)

    weight = 1.0 / (1.0 + jnp.exp(-gap(logits)))
    weight_tan = weight * (1.0 - weight) * gap(logit_tan)
    spot = lax.broadcasted_iota(jnp.int32, (rows, span), 1)
    for batch in range(BATCHES):
        expert = expert_of(spot // (2 * cap), batch)
        is_one, is_two = one == expert, second == expert
        named = is_one | is_two
        rank = jnp.dot(late, named.astype(F32).astype(BF16), preferred_element_type=F32)
        chosen = named & (rank == (spot % cap).astype(F32))
        is_main = (spot % (2 * cap)) < cap
        share = jnp.where(is_one, weight, 1.0 - weight)
        share_tan = jnp.where(is_one, weight_tan, -weight_tan)
        for first, value in (
            (0, jnp.where(chosen & is_main, share, 0.0)),
            (rows, jnp.where(chosen, jnp.where(is_main, share_tan, share), 0.0)),
        ):
            high = value.astype(BF16)
            mix_hi[batch, pl.ds(first, rows)] = high
            mix_lo[batch, pl.ds(first, rows)] = (value - high.astype(F32)).astype(BF16)

    def spread_weights(a, k, kind):
        at_core, place = HOME[kind]
        rows_in = pl.ds(k * step[a], step[a])
        src = far[a].at[rows_in] if kind == FAR else near[a].at[kind, rows_in]
        dst = held[a].at[place, pl.ds(dp * part[a] + k * step[a], step[a])]
        sems = a * CHUNKS + k
        rest = rest_sem.at[place, a]

        @pl.when(core == at_core)
        def _():
            pltpu.make_async_copy(src, dst, rest).start()

        @pl.when(core != at_core)
        def _():
            remote(src, dst, spread_send.at[kind, a], rest, device(0, at_core, x, 0)).start()

        @pl.when(core == 0)
        def _():
            remote(src, dst, spread_send.at[kind, a], first_sem.at[place, sems, 0], device(1, at_core, x, 0)).start()
            remote(src, dst, spread_send.at[kind, a], rest, device(-1, at_core, x, 0)).start()

        @pl.when(core == 1)
        def _():
            remote(src, dst, spread_send.at[kind, a], rest, device(1, at_core, x, 0)).start()
            remote(src, dst, spread_send.at[kind, a], first_sem.at[place, sems, 1], device(-1, at_core, x, 0)).start()

    def pass_weights(a, k, place):
        for side, dy in ((0, 1), (1, -1)):
            piece = ((y - dy + Y) % Y) * 2 + side
            ref = held[a].at[place, pl.ds(piece * part[a] + k * step[a], step[a])]
            wait_bytes(ref, first_sem.at[place, a * CHUNKS + k, side])
            remote(ref, ref, pass_send.at[place, a], rest_sem.at[place, a], device(dy, core, x, 0)).start()

    def work(batch):
        group, place = batch // 2, batch % 2
        blocks = pl.ds(batch * BLOCKS, BLOCKS)
        wait_bytes(rx.at[blocks], recv_sem.at[batch])

        @pl.loop(0, hidden_width // 256)
        def _(n):
            cols = pl.ds(pl.multiple_of(n * 256, 256), 256)
            both = jnp.dot(
                rx[blocks].reshape(span, width), wbi[place, :, cols], preferred_element_type=F32
            ).reshape(BLOCKS, 2 * cap, 256)
            hidden = both[:, :cap] + bias_in[pl.ds(place, 1), cols].reshape(1, 1, 256)
            hidden_tan = both[:, cap:]
            tanh_val = jnp.tanh(gelu_scale * (hidden + cubic_coef * hidden * hidden * hidden))
            hid[:, pl.ds(0, cap), cols] = (0.5 * hidden * (1.0 + tanh_val)).astype(BF16)
            slope = 0.5 * (1.0 + tanh_val) + 0.5 * hidden * (1.0 - tanh_val * tanh_val) * gelu_scale * (
                1.0 + 3.0 * cubic_coef * hidden * hidden
            )
            hid[:, pl.ds(cap, cap), cols] = (slope * hidden_tan).astype(BF16)

        @pl.loop(0, width // 512)
        def _(n):
            cols = pl.ds(pl.multiple_of(n * 512, 512), 512)
            both = jnp.dot(
                hid[...].reshape(span, hidden_width), wbo[place, :, cols], preferred_element_type=F32
            ).reshape(BLOCKS, 2 * cap, 512)
            rx[blocks, pl.ds(0, cap), cols] = (
                both[:, :cap] + bias_out[pl.ds(place, 1), cols].reshape(1, 1, 512)).astype(BF16)
            rx[blocks, pl.ds(cap, cap), cols] = both[:, cap:].astype(BF16)

        for dx in range(X):
            to_x = (x + dx) % X
            dz = -group * (1 - 2 * (dx % 2))
            for c in range(2):
                to_core = (core + c) % 2
                src = rx.at[batch * BLOCKS + to_x * 2 + to_core]
                dst = back.at[batch * BLOCKS + mine]
                if (dx, dz, c) == (0, 0, 0):
                    pltpu.make_async_copy(src, dst, ret_recv.at[batch]).start()
                else:
                    remote(src, dst, ret_send.at[0], ret_recv.at[batch], device(0, to_core, to_x, dz)).start()

    def wait_rest(place):
        for a in range(2):
            wait_bytes(held[a].at[place, pl.ds(0, 6 * part[a])], rest_sem.at[place, a])

    for a, k in units:
        for kind in (UP, DOWN):
            near_copy(a, k, kind).wait_recv()
        far_copy(a, k).start()
        for kind in (UP, DOWN):
            spread_weights(a, k, kind)

    for copy in biases:
        copy.wait()
    for bias, own, up, low, away in (
        (bias_in, b_in, bi_up, bi_down, bi_far), (bias_out, b_out, bo_up, bo_down, bo_far)
    ):
        bias[pl.ds(0, 1)] = jnp.where(core == 0, own[...], up[...])
        bias[pl.ds(1, 1)] = jnp.where(core == 0, away[...], low[...])

    @pl.when(core == 1)
    def _():
        for a, k in units:
            for place in range(2):
                pass_weights(a, k, place)

    for a, k in units:
        far_copy(a, k).wait_recv()
        spread_weights(a, k, FAR)

    @pl.when(core == 0)
    def _():
        wait_bytes(wbi.at[0], own_sem.at[0])
        wait_bytes(wbo.at[0], own_sem.at[1])

    @pl.when(core == 1)
    def _():
        wait_rest(0)

    work(WORK_ORDER[0])
    work(WORK_ORDER[1])

    @pl.when(core == 0)
    def _():
        for a, k in units:
            pass_weights(a, k, 1)

    wait_rest(1)
    work(WORK_ORDER[2])
    work(WORK_ORDER[3])

    for order, batch in enumerate(WORK_ORDER):
        blocks = pl.ds(batch * BLOCKS, BLOCKS)
        wait_bytes(back.at[blocks], ret_recv.at[batch])

        @pl.loop(0, width // 512)
        def _(n, order=order, batch=batch, blocks=blocks):
            cols = pl.ds(pl.multiple_of(n * 512, 512), 512)
            parts = back[blocks, :, cols].reshape(span, 512)
            mixed = jnp.dot(mix_hi[batch], parts, preferred_element_type=F32) + jnp.dot(
                mix_lo[batch], parts, preferred_element_type=F32)
            if order > 0:
                mixed = mixed + acc[:, cols]
            if order < BATCHES - 1:
                acc[:, cols] = mixed
            else:
                gate, gate_tan = mods[pl.ds(2, 1), cols], mods[pl.ds(5, 1), cols]
                mixture, mixture_tan = mixed[:rows], mixed[rows:]
                out[:, cols] = (tok[:, cols].astype(F32) + gate * mixture).astype(BF16)
                out_tan[:, cols] = (
                    tan[:, cols].astype(F32) + gate_tan * mixture + gate * mixture_tan).astype(BF16)

    wait_bytes(tx.at[pl.ds(0, SLOTS - 2)], send_sem.at[0])
    wait_bytes(rx.at[pl.ds(0, SLOTS - 2)], ret_send.at[0])
    for a in range(2):
        wait_bytes(held[a].at[0, pl.ds(0, 2 * part[a])], near_send.at[a])
        wait_bytes(held[a].at[0, pl.ds(0, part[a])], far_send.at[a])
        for kind in (UP, DOWN, FAR):
            @pl.when(core == HOME[kind][0])
            def _(a=a, kind=kind):
                wait_bytes(held[a].at[0, pl.ds(0, 2 * part[a])], spread_send.at[kind, a])

            @pl.when(core != HOME[kind][0])
            def _(a=a, kind=kind):
                wait_bytes(held[a].at[0, pl.ds(0, 3 * part[a])], spread_send.at[kind, a])

        @pl.when(core == 1)
        def _(a=a):
            wait_bytes(held[a].at[0, pl.ds(0, 2 * part[a])], pass_send.at[0, a])

        wait_bytes(held[a].at[0, pl.ds(0, 2 * part[a])], pass_send.at[1, a])


def local(tokens, tangent, bucket, mod_table, mod_rate, router, routes, w_in, b_in, w_out, b_out):
    rows, width = tokens.shape
    hidden_width = w_in.shape[2]
    cap = 4 * rows // router.shape[1]
    parts = lax.axis_size("dp")
    vmem = pl.BlockSpec(memory_space=pltpu.VMEM)
    smem = pl.BlockSpec(memory_space=pltpu.SMEM)
    hbm = pl.BlockSpec(memory_space=pl.ANY)
    shape = jax.ShapeDtypeStruct((rows, width), BF16)
    dma = pltpu.SemaphoreType.DMA
    units = 2 * CHUNKS
    blocks = pltpu.VMEM((SLOTS, 2 * cap, width), BF16)
    mix = pltpu.VMEM((BATCHES, 2 * rows, BLOCKS * 2 * cap), BF16)
    return tuple(pl.pallas_call(
        kernel,
        out_shape=(shape, shape),
        in_specs=[vmem, vmem, smem, vmem, vmem, vmem, vmem, hbm, vmem, hbm, vmem],
        out_specs=(vmem, vmem),
        scratch_shapes=[
            pltpu.VMEM((rows, width), BF16),
            pltpu.VMEM((rows, width), BF16),
            blocks, blocks, blocks,
            pltpu.VMEM((2 * rows, width), F32),
            mix, mix,
            pltpu.VMEM((BLOCKS, 2 * cap, hidden_width), BF16),
            pltpu.VMEM((8, width), F32),
            pltpu.VMEM((2, width, hidden_width), BF16),
            pltpu.VMEM((2, hidden_width, width), BF16),
            pltpu.VMEM((2, width // parts, hidden_width), BF16),
            pltpu.VMEM((2, hidden_width // parts, width), BF16),
            pltpu.VMEM((width // parts, hidden_width), BF16),
            pltpu.VMEM((hidden_width // parts, width), BF16),
            pltpu.VMEM((2, hidden_width), F32),
            pltpu.VMEM((2, width), F32),
            *[pltpu.VMEM((1, hidden_width), F32)] * 3,
            *[pltpu.VMEM((1, width), F32)] * 3,
            dma((1,)), dma((BATCHES,)), dma((1,)), dma((BATCHES,)), dma((2,)),
            dma((2,)), dma((2, units)), dma((2,)), dma((units,)),
            dma((3, 2)), dma((2, 2)), dma((2, units, 2)), dma((2, 2)), dma((2, 3)), dma((2, 3)),
        ],
        compiler_params=pltpu.CompilerParams(
            collective_id=0, has_side_effects=True, vmem_limit_bytes=60 << 20),
    )(tokens, tangent, bucket, mod_table.transpose(1, 0, 2), mod_rate.transpose(1, 0, 2), router.T, routes.T,
      w_in, b_in, w_out, b_out))


def solution(mesh):
    in_specs = (
        P(("dp", "seq"), None),
        P(("dp", "seq"), None),
        P("dp"),
        P(),
        P(),
        P(),
        P(("dp", "seq"), None),
        P("seq", None, None),
        P("seq", None),
        P("seq", None, None),
        P("seq", None),
    )
    out_specs = (P(("dp", "seq"), None), P(("dp", "seq"), None))
    return jax.shard_map(local, mesh=mesh, in_specs=in_specs, out_specs=out_specs, check_vma=False)
```

time: 273 us -> 225 us (0.82); the launches traced: 269 us -> 223 us
  Pallas kernels: 256 us -> 218 us
  local copies, waits for them, and re-layouts: 11.1 us -> 4.13 us
    pallas_call x1, Pallas kernels: 256 us -> 218 us  [local(): pl.pallas_call(kernel, out_shape=(shape, shape), in_specs=[vmem, vmem, sm...]
    unnamed x6 -> x2, local copies, waits for them, and re-layouts: 11.1 us -> 4.13 us
where the time goes in v2:
time: 225 us; the launch traced here: 223 us
  Pallas kernels  218 us (97%)
  local copies, waits for them, and re-layouts  4.13 us (2%)
    pallas_call x1, Pallas kernels, local(): pl.pallas_call(kernel, out_shape=(shape, shape), in_specs=[vmem, vmem, sm...  218 us

profile of v2, /device:TPU:1, one launch (start us, length us, event | category | flops | bytes accessed | tf_op | source)
XLA Modules:
  0.0 223.5 jit_solution(5833225883250575581)
XLA Ops:
  1.3 218.1 %shard_map.122 = (bf16[128,3072]{1,0:T(8,128)(2,1)}, bf16[128,3072]{1,0:T(8,128)(2,1)}) custom-call(bf16[128,3072]{1,0:T(8,128)(2,1)} %tok.1, bf16[128,3072]{1,0:T(8,128)(2,1)} %tan.1, s32[1]{0:T(128)S(6)} %copy.15.bucket, bf16[3,8,3072]{2,1,0:T(8,128)(2,1)} %bitcast.5, bf16[3,8,3072]{2,1,0:T(8,128)(2,1)} %bitcast.6, bf16[32,3072]{1,0:T(8,128)(2,1)} %bitcast.4, ...), custom_call_target="tpu_custom_call" | custom-call | tf_op jit(solution)/shard_map/pallas_call | solution.py:373
  219.4 2.1 copy.16
  221.4 2.1 copy.17

commit v3 on v2

v3 whole, which is shorter than its diff:
```python
import jax
import jax.numpy as jnp
from jax import lax
from jax.experimental import pallas as pl
from jax.experimental.pallas import tpu as pltpu
from jax.sharding import PartitionSpec as P

norm_eps = 1e-06
gelu_scale = 0.7978845608
cubic_coef = 0.044715

MESH = pl.DeviceIdType.MESH
F32 = jnp.float32
BF16 = jnp.bfloat16

X, Y, Z = 4, 4, 8
SIZES = (12, 8, 8, 4)
FIRST = (0, 12, 20, 28)
SLOTS = 32
SEND_ORDER = (0, 1, 3, 2)
HELD_BACK = (3, 2)
WORK_ORDER = (1, 2, 3)
CHUNKS = 2
WINDOW = 2
EARLY = 3
TOKENS_AT = 3
UP, DOWN = 0, 1


def wait_bytes(ref, sem):
    pltpu.make_async_copy(ref, ref, sem).wait()


def kernel(
    tok, tan, bucket, table, rate, router, routes_t, w_in, b_in, w_out, b_out,
    out, out_tan,
    modded, modded_tan, tx, rx, back, acc, mix_hi, mix_lo, hid, mods, wbi, wbo, near_in, near_out,
    bias_in, bias_out, bi_up, bi_down, bo_up, bo_down,
    send_sem, recv_sem, ret_send, ret_recv, own_sem, near_send, near_recv,
    spread_send, rest_sem, first_sem, pass_send, bias_send, bias_recv,
):
    rows, width = tok.shape
    cap = tx.shape[1] // 2
    hidden_width = wbi.shape[2]
    dp, seq = lax.axis_index("dp"), lax.axis_index("seq")
    y, core = dp // 2, dp % 2
    x, z = seq // Z, seq % Z

    def device(dy, c, to_x, dz):
        return {"dp": ((y + dy + Y) % Y) * 2 + c, "seq": to_x * Z + (z + dz + Z) % Z}

    def remote(src, dst, send, recv, to):
        return pltpu.make_async_remote_copy(src, dst, send, recv, device_id=to, device_id_type=MESH)

    barrier = pltpu.get_barrier_semaphore()
    peers = [
        device(0, (core + dc) % 2, (x + dx) % X, dz)
        for dz in (0, 1, -1, 2, -2) for dx in range(X) for dc in range(2)
        if (dz, dx, dc) != (0, 0, 0)
    ]
    peers += [device(dy, c, x, 0) for dy in (1, -1) for c in range(2)]
    for peer in peers:
        pl.semaphore_signal(barrier, inc=1, device_id=peer, device_id_type=MESH)
    pl.semaphore_wait(barrier, len(peers))

    part = (near_in.shape[1], near_out.shape[1])
    step = (part[0] // CHUNKS, part[1] // CHUNKS)
    units = [(a, k) for a in range(2) for k in range(CHUNKS)]
    near, full, held = (near_in, near_out), (w_in, w_out), (wbi, wbo)

    def near_copy(a, k, kind):
        return remote(
            full[a].at[0, pl.ds(dp * part[a] + k * step[a], step[a])],
            near[a].at[kind, pl.ds(k * step[a], step[a])],
            near_send.at[a], near_recv.at[kind, a * CHUNKS + k],
            device(0, core, x, -2 if kind == UP else 2))

    biases = []
    for kind, dz, to_in, to_out in ((UP, -2, bi_up, bo_up), (DOWN, 2, bi_down, bo_down)):
        to = device(0, core, x, dz)
        biases.append(remote(b_in, to_in, bias_send.at[0, kind], bias_recv.at[0, kind], to))
        biases.append(remote(b_out, to_out, bias_send.at[1, kind], bias_recv.at[1, kind], to))
    for a, k in units[:WINDOW]:
        for kind in (UP, DOWN):
            near_copy(a, k, kind).start()
    for copy in biases:
        copy.start()

    pltpu.make_async_copy(w_in.at[0], wbi.at[0], own_sem.at[0]).start()
    pltpu.make_async_copy(w_out.at[0], wbo.at[0], own_sem.at[1]).start()

    at_row = lax.broadcasted_iota(jnp.int32, (table.shape[1], width), 0) == bucket[0]
    for k in range(3):
        for first, source in ((0, table), (3, rate)):
            mods[pl.ds(first + k, 1)] = jnp.sum(
                jnp.where(at_row, source[k].astype(F32), 0.0), axis=0, keepdims=True)
    offset, offset_tan = mods[pl.ds(0, 1)], mods[pl.ds(3, 1)]
    scale, scale_tan = 1.0 + mods[pl.ds(1, 1)], mods[pl.ds(4, 1)]

    @pl.loop(0, rows // 16)
    def _(i):
        at = pl.ds(pl.multiple_of(i * 16, 16), 16)
        values = tok[at].astype(F32)
        deltas = tan[at].astype(F32)
        center = values - jnp.mean(values, axis=-1, keepdims=True)
        spread = jnp.mean(center * center, axis=-1, keepdims=True)
        inverse = lax.rsqrt(spread + norm_eps)
        normed = center * inverse
        normed_tan = (
            deltas
            - jnp.mean(deltas, axis=-1, keepdims=True)
            - normed * jnp.mean(normed * deltas, axis=-1, keepdims=True)
        ) * inverse
        modded[at] = (normed * scale + offset).astype(BF16)
        modded_tan[at] = (normed_tan * scale + normed * scale_tan + offset_tan).astype(BF16)

    def expert_of(block, batch):
        if batch == 0:
            to_x, move = block % X, block // X - 3 * (block // (2 * X))
        elif batch == 3:
            to_x, move = block, 4
        else:
            to_x, move = block // 2, (batch + 1) * (1 - 2 * (block % 2))
        return to_x * Z + (z + move + Z) % Z

    def out_legs(batch):
        first = FIRST[batch]
        for dx in range(X):
            to_x = (x + dx) % X
            if batch == 0:
                for k, dz in enumerate((0, 1, -1)):
                    yield first + k * X + to_x, first + k * X + x, device(0, core, to_x, dz), (dx, k) == (0, 0)
            elif batch == 3:
                side = dx % 2
                yield first + to_x, first + x // 2 * 2 + core, device(0, side, to_x, 2 - 4 * side), False
            else:
                for c in range(2):
                    side = (core + c) % 2
                    dz = (batch - 1) * (1 - 2 * side)
                    yield (first + to_x * 2 + side, first + x * 2 + core, device(0, side, to_x, dz),
                           (batch, dx, c) == (1, 0, 0))

    def home_legs(batch):
        first = FIRST[batch]
        sign = 1 - 2 * core
        if batch == 3:
            for h in range(2):
                to_x = 2 * h + (x + core) % 2
                for c in range(2):
                    yield first + 2 * h + c, first + x, device(0, c, to_x, -2 * sign), False
            return
        for dx in range(X):
            to_x = (x + dx) % X
            if batch == 0:
                for k, dz in enumerate((0, 1, -1)):
                    yield first + k * X + to_x, first + k * X + x, device(0, core, to_x, -dz), (dx, k) == (0, 0)
            else:
                for c in range(2):
                    side = (core + c) % 2
                    yield (first + to_x * 2 + side, first + x * 2 + core,
                           device(0, side, to_x, -(batch - 1) * sign), (batch, dx, c) == (1, 0, 0))

    def send_out(batch):
        for here, there, to, own in out_legs(batch):
            if own:
                pltpu.make_async_copy(tx.at[here], rx.at[there], recv_sem.at[batch]).start()
            else:
                remote(tx.at[here], rx.at[there], send_sem.at[0], recv_sem.at[batch], to).start()

    one_t, two_t = routes_t[0:1], routes_t[1:2]
    square = (rows, rows)
    down, across = lax.broadcasted_iota(jnp.int32, square, 0), lax.broadcasted_iota(jnp.int32, square, 1)
    early = (down < across).astype(F32).astype(BF16)
    late = (across < down).astype(F32).astype(BF16)
    for batch in SEND_ORDER:
        size = SIZES[batch]
        line = lax.broadcasted_iota(jnp.int32, (size * cap, rows), 0)
        expert = expert_of(line // cap, batch)
        named = (one_t == expert) | (two_t == expert)
        rank = jnp.dot(named.astype(F32).astype(BF16), early, preferred_element_type=F32)
        pick = (named & (rank == (line % cap).astype(F32))).astype(F32).astype(BF16)

        @pl.loop(0, width // 512)
        def _(n, batch=batch, size=size, pick=pick):
            cols = pl.ds(pl.multiple_of(n * 512, 512), 512)
            for source, first in ((modded, 0), (modded_tan, cap)):
                packed = jnp.dot(pick, source[:, cols], preferred_element_type=F32).astype(BF16)
                tx[pl.ds(FIRST[batch], size), pl.ds(first, cap), cols] = packed.reshape(size, cap, 512)

        if batch not in HELD_BACK:
            send_out(batch)

    turn = (((1,), (1,)), ((), ()))
    logits = lax.dot_general(modded[...], router[...], turn, preferred_element_type=F32)
    logit_tan = lax.dot_general(modded_tan[...], router[...], turn, preferred_element_type=F32)
    one = jnp.sum(jnp.where(down == across, one_t, 0).astype(F32), axis=1, keepdims=True).astype(jnp.int32)
    second = jnp.sum(jnp.where(down == across, two_t, 0).astype(F32), axis=1, keepdims=True).astype(jnp.int32)
    lane = lax.broadcasted_iota(jnp.int32, logits.shape, 1)

    def gap(values):
        return jnp.sum(jnp.where(lane == one, values, 0.0), axis=1, keepdims=True) - jnp.sum(
            jnp.where(lane == second, values, 0.0), axis=1, keepdims=True)

    weight = 1.0 / (1.0 + jnp.exp(-gap(logits)))
    weight_tan = weight * (1.0 - weight) * gap(logit_tan)
    for batch, size in enumerate(SIZES):
        spot = lax.broadcasted_iota(jnp.int32, (rows, size * 2 * cap), 1)
        cols = pl.ds(FIRST[batch] * 2 * cap, size * 2 * cap)
        expert = expert_of(spot // (2 * cap), batch)
        is_one, is_two = one == expert, second == expert
        named = is_one | is_two
        rank = jnp.dot(late, named.astype(F32).astype(BF16), preferred_element_type=F32)
        chosen = named & (rank == (spot % cap).astype(F32))
        is_main = (spot % (2 * cap)) < cap
        share = jnp.where(is_one, weight, 1.0 - weight)
        share_tan = jnp.where(is_one, weight_tan, -weight_tan)
        for first, value in (
            (0, jnp.where(chosen & is_main, share, 0.0)),
            (rows, jnp.where(chosen, jnp.where(is_main, share_tan, share), 0.0)),
        ):
            high = value.astype(BF16)
            mix_hi[pl.ds(first, rows), cols] = high
            mix_lo[pl.ds(first, rows), cols] = (value - high.astype(F32)).astype(BF16)

    def spread_weights(a, k, kind):
        src = near[a].at[kind, pl.ds(k * step[a], step[a])]
        dst = held[a].at[1, pl.ds(dp * part[a] + k * step[a], step[a])]
        unit = a * CHUNKS + k
        send, rest = spread_send.at[kind, a], rest_sem.at[a]

        @pl.when(core == kind)
        def _():
            pltpu.make_async_copy(src, dst, rest).start()

        @pl.when(core != kind)
        def _():
            remote(src, dst, send, rest, device(0, kind, x, 0)).start()

        @pl.when(core == 0)
        def _():
            remote(src, dst, send, first_sem.at[unit, 0], device(1, kind, x, 0)).start()
            remote(src, dst, send, rest, device(-1, kind, x, 0)).start()

        @pl.when(core == 1)
        def _():
            remote(src, dst, send, rest, device(1, kind, x, 0)).start()
            remote(src, dst, send, first_sem.at[unit, 1], device(-1, kind, x, 0)).start()

    def pass_weights(a, k):
        for side, dy in ((0, 1), (1, -1)):
            piece = ((y - dy + Y) % Y) * 2 + side
            ref = held[a].at[1, pl.ds(piece * part[a] + k * step[a], step[a])]
            wait_bytes(ref, first_sem.at[a * CHUNKS + k, side])
            remote(ref, ref, pass_send.at[a], rest_sem.at[a], device(dy, core, x, 0)).start()

    def work(batch):
        place, size = min(batch, 1), SIZES[batch]
        span = size * 2 * cap
        blocks = pl.ds(FIRST[batch], size)
        wait_bytes(rx.at[blocks], recv_sem.at[batch])

        @pl.loop(0, hidden_width // 256)
        def _(n):
            cols = pl.ds(pl.multiple_of(n * 256, 256), 256)
            both = jnp.dot(
                rx[blocks].reshape(span, width), wbi[place, :, cols], preferred_element_type=F32
            ).reshape(size, 2 * cap, 256)
            hidden = both[:, :cap] + bias_in[pl.ds(place, 1), cols].reshape(1, 1, 256)
            hidden_tan = both[:, cap:]
            tanh_val = jnp.tanh(gelu_scale * (hidden + cubic_coef * hidden * hidden * hidden))
            hid[pl.ds(0, size), pl.ds(0, cap), cols] = (0.5 * hidden * (1.0 + tanh_val)).astype(BF16)
            slope = 0.5 * (1.0 + tanh_val) + 0.5 * hidden * (1.0 - tanh_val * tanh_val) * gelu_scale * (
                1.0 + 3.0 * cubic_coef * hidden * hidden
            )
            hid[pl.ds(0, size), pl.ds(cap, cap), cols] = (slope * hidden_tan).astype(BF16)

        @pl.loop(0, width // 512)
        def _(n):
            cols = pl.ds(pl.multiple_of(n * 512, 512), 512)
            both = jnp.dot(
                hid[pl.ds(0, size)].reshape(span, hidden_width), wbo[place, :, cols], preferred_element_type=F32
            ).reshape(size, 2 * cap, 512)
            rx[blocks, pl.ds(0, cap), cols] = (
                both[:, :cap] + bias_out[pl.ds(place, 1), cols].reshape(1, 1, 512)).astype(BF16)
            rx[blocks, pl.ds(cap, cap), cols] = both[:, cap:].astype(BF16)

        for here, there, to, own in home_legs(batch):
            if own:
                pltpu.make_async_copy(rx.at[here], back.at[there], ret_recv.at[batch]).start()
            else:
                remote(rx.at[here], back.at[there], ret_send.at[0], ret_recv.at[batch], to).start()

    for copy in biases:
        copy.wait()
    for bias, own, up, low in ((bias_in, b_in, bi_up, bi_down), (bias_out, b_out, bo_up, bo_down)):
        bias[pl.ds(0, 1)] = own[...]
        bias[pl.ds(1, 1)] = jnp.where(core == 0, up[...], low[...])

    def own_work():
        wait_bytes(wbi.at[0], own_sem.at[0])
        wait_bytes(wbo.at[0], own_sem.at[1])
        work(0)

    for u, (a, k) in enumerate(units):
        for kind in (UP, DOWN):
            near_copy(a, k, kind).wait_recv()
        if u + WINDOW < len(units):
            for kind in (UP, DOWN):
                near_copy(*units[u + WINDOW], kind).start()
        for kind in (UP, DOWN):
            spread_weights(a, k, kind)
        if u == TOKENS_AT:
            for batch in HELD_BACK:
                send_out(batch)
        if u > 0:
            pass_weights(*units[u - 1])
        if u == EARLY:
            own_work()
    pass_weights(*units[-1])
    if EARLY >= len(units):
        own_work()
    for a in range(2):
        wait_bytes(held[a].at[1, pl.ds(0, 6 * part[a])], rest_sem.at[a])
    for batch in WORK_ORDER:
        work(batch)

    for order, batch in enumerate((0,) + WORK_ORDER):
        blocks = pl.ds(FIRST[batch], SIZES[batch])
        wait_bytes(back.at[blocks], ret_recv.at[batch])
        span = SIZES[batch] * 2 * cap
        spots = pl.ds(FIRST[batch] * 2 * cap, span)

        @pl.loop(0, width // 512)
        def _(n, order=order, blocks=blocks, span=span, spots=spots):
            cols = pl.ds(pl.multiple_of(n * 512, 512), 512)
            parts = back[blocks, :, cols].reshape(span, 512)
            mixed = jnp.dot(mix_hi[:, spots], parts, preferred_element_type=F32) + jnp.dot(
                mix_lo[:, spots], parts, preferred_element_type=F32)
            if order > 0:
                mixed = mixed + acc[:, cols]
            if order < len(WORK_ORDER):
                acc[:, cols] = mixed
            else:
                gate, gate_tan = mods[pl.ds(2, 1), cols], mods[pl.ds(5, 1), cols]
                mixture, mixture_tan = mixed[:rows], mixed[rows:]
                out[:, cols] = (tok[:, cols].astype(F32) + gate * mixture).astype(BF16)
                out_tan[:, cols] = (
                    tan[:, cols].astype(F32) + gate_tan * mixture + gate * mixture_tan).astype(BF16)

    wait_bytes(tx.at[pl.ds(0, SLOTS - 2)], send_sem.at[0])
    wait_bytes(rx.at[pl.ds(0, SLOTS - 2)], ret_send.at[0])
    for a in range(2):
        wait_bytes(held[a].at[0, pl.ds(0, 2 * part[a])], near_send.at[a])
        for kind in (UP, DOWN):
            @pl.when(core == kind)
            def _(a=a, kind=kind):
                wait_bytes(held[a].at[0, pl.ds(0, 2 * part[a])], spread_send.at[kind, a])

            @pl.when(core != kind)
            def _(a=a, kind=kind):
                wait_bytes(held[a].at[0, pl.ds(0, 3 * part[a])], spread_send.at[kind, a])

        wait_bytes(held[a].at[0, pl.ds(0, 2 * part[a])], pass_send.at[a])


def local(tokens, tangent, bucket, mod_table, mod_rate, router, routes, w_in, b_in, w_out, b_out):
    rows, width = tokens.shape
    hidden_width = w_in.shape[2]
    cap = 4 * rows // router.shape[1]
    parts = lax.axis_size("dp")
    vmem = pl.BlockSpec(memory_space=pltpu.VMEM)
    smem = pl.BlockSpec(memory_space=pltpu.SMEM)
    hbm = pl.BlockSpec(memory_space=pl.ANY)
    shape = jax.ShapeDtypeStruct((rows, width), BF16)
    dma = pltpu.SemaphoreType.DMA
    units = 2 * CHUNKS
    blocks = pltpu.VMEM((SLOTS, 2 * cap, width), BF16)
    mix = pltpu.VMEM((2 * rows, SLOTS * 2 * cap), BF16)
    return tuple(pl.pallas_call(
        kernel,
        out_shape=(shape, shape),
        in_specs=[vmem, vmem, smem, vmem, vmem, vmem, vmem, hbm, vmem, hbm, vmem],
        out_specs=(vmem, vmem),
        scratch_shapes=[
            pltpu.VMEM((rows, width), BF16),
            pltpu.VMEM((rows, width), BF16),
            blocks, blocks, blocks,
            pltpu.VMEM((2 * rows, width), F32),
            mix, mix,
            pltpu.VMEM((max(SIZES), 2 * cap, hidden_width), BF16),
            pltpu.VMEM((8, width), F32),
            pltpu.VMEM((2, width, hidden_width), BF16),
            pltpu.VMEM((2, hidden_width, width), BF16),
            pltpu.VMEM((2, width // parts, hidden_width), BF16),
            pltpu.VMEM((2, hidden_width // parts, width), BF16),
            pltpu.VMEM((2, hidden_width), F32),
            pltpu.VMEM((2, width), F32),
            *[pltpu.VMEM((1, hidden_width), F32)] * 2,
            *[pltpu.VMEM((1, width), F32)] * 2,
            dma((1,)), dma((len(SIZES),)), dma((1,)), dma((len(SIZES),)), dma((2,)),
            dma((2,)), dma((2, units)),
            dma((2, 2)), dma((2,)), dma((units, 2)), dma((2,)), dma((2, 2)), dma((2, 2)),
        ],
        compiler_params=pltpu.CompilerParams(
            collective_id=0, has_side_effects=True, vmem_limit_bytes=60 << 20),
    )(tokens, tangent, bucket, mod_table.transpose(1, 0, 2), mod_rate.transpose(1, 0, 2), router.T, routes.T,
      w_in, b_in, w_out, b_out))


def solution(mesh):
    in_specs = (
        P(("dp", "seq"), None),
        P(("dp", "seq"), None),
        P("dp"),
        P(),
        P(),
        P(),
        P(("dp", "seq"), None),
        P("seq", None, None),
        P("seq", None),
        P("seq", None, None),
        P("seq", None),
    )
    out_specs = (P(("dp", "seq"), None), P(("dp", "seq"), None))
    return jax.shard_map(local, mesh=mesh, in_specs=in_specs, out_specs=out_specs, check_vma=False)
```

time: 225 us -> 212 us (0.942)
  Pallas kernels: 218 us -> 206 us
    pallas_call x1, Pallas kernels: 218 us -> 206 us  [local(): pl.pallas_call(kernel, out_shape=(shape, shape), in_specs=[vmem, vmem, sm...]
where the time goes in v3:
time: 212 us
  Pallas kernels  206 us (97%)
  local copies, waits for them, and re-layouts  4.13 us (2%)
    pallas_call x1, Pallas kernels, local(): pl.pallas_call(kernel, out_shape=(shape, shape), in_specs=[vmem, vmem, sm...  206 us

profile of v3, /device:TPU:1, one launch (start us, length us, event | category | flops | bytes accessed | tf_op | source)
XLA Modules:
  0.0 211.9 jit_solution(12778546729523490648)
XLA Ops:
  1.3 206.5 %shard_map.122 = (bf16[128,3072]{1,0:T(8,128)(2,1)}, bf16[128,3072]{1,0:T(8,128)(2,1)}) custom-call(bf16[128,3072]{1,0:T(8,128)(2,1)} %tok.1, bf16[128,3072]{1,0:T(8,128)(2,1)} %tan.1, s32[1]{0:T(128)S(6)} %copy.15.bucket, bf16[3,8,3072]{2,1,0:T(8,128)(2,1)} %bitcast.5, bf16[3,8,3072]{2,1,0:T(8,128)(2,1)} %bitcast.6, bf16[32,3072]{1,0:T(8,128)(2,1)} %bitcast.4, ...), custom_call_target="tpu_custom_call" | custom-call | tf_op jit(solution)/shard_map/pallas_call | solution.py:379
  207.8 2.1 copy.16
  209.8 2.1 copy.17

commit v4 on v3

--- a/solution.py
+++ b/solution.py
@@ -17,13 +17,11 @@
 SIZES = (12, 8, 8, 4)
 FIRST = (0, 12, 20, 28)
 SLOTS = 32
-SEND_ORDER = (0, 1, 3, 2)
-HELD_BACK = (3, 2)
 WORK_ORDER = (1, 2, 3)
 CHUNKS = 2
 WINDOW = 2
 EARLY = 3
-TOKENS_AT = 3
+RELAY_AT = 1
 UP, DOWN = 0, 1
 
 
@@ -34,10 +32,10 @@
 def kernel(
     tok, tan, bucket, table, rate, router, routes_t, w_in, b_in, w_out, b_out,
     out, out_tan,
-    modded, modded_tan, tx, rx, back, acc, mix_hi, mix_lo, hid, mods, wbi, wbo, near_in, near_out,
+    modded, modded_tan, around, routes_around, tx, rx, back, acc, mix_hi, mix_lo, hid, mods, wbi, wbo, near_in, near_out,
     bias_in, bias_out, bi_up, bi_down, bo_up, bo_down,
     send_sem, recv_sem, ret_send, ret_recv, own_sem, near_send, near_recv,
-    spread_send, rest_sem, first_sem, pass_send, bias_send, bias_recv,
+    around_send, around_recv, routes_recv, spread_send, rest_sem, first_sem, pass_send, bias_send, bias_recv,
 ):
     rows, width = tok.shape
     cap = tx.shape[1] // 2
@@ -83,7 +81,11 @@
     for a, k in units[:WINDOW]:
         for kind in (UP, DOWN):
             near_copy(a, k, kind).start()
-    for copy in biases:
+    route_copies = [
+        remote(routes_t, routes_around.at[side], around_send.at[1 + side], routes_recv.at[side], device(0, core, x, dz))
+        for side, dz in ((0, 1), (1, -1))
+    ]
+    for copy in biases + route_copies:
         copy.start()
 
     pltpu.make_async_copy(w_in.at[0], wbi.at[0], own_sem.at[0]).start()
@@ -123,22 +125,22 @@
             to_x, move = block // 2, (batch + 1) * (1 - 2 * (block % 2))
         return to_x * Z + (z + move + Z) % Z
 
-    def out_legs(batch):
+    def out_legs(batch, parts):
         first = FIRST[batch]
         for dx in range(X):
             to_x = (x + dx) % X
             if batch == 0:
-                for k, dz in enumerate((0, 1, -1)):
-                    yield first + k * X + to_x, first + k * X + x, device(0, core, to_x, dz), (dx, k) == (0, 0)
+                for k in range(3):
+                    if k in parts:
+                        yield first + k * X + to_x, first + k * X + x, device(0, core, to_x, 0), dx == 0
             elif batch == 3:
                 side = dx % 2
-                yield first + to_x, first + x // 2 * 2 + core, device(0, side, to_x, 2 - 4 * side), False
+                yield first + to_x, first + x // 2 * 2 + core, device(0, side, to_x, 1 - 2 * side), False
             else:
                 for c in range(2):
                     side = (core + c) % 2
-                    dz = (batch - 1) * (1 - 2 * side)
-                    yield (first + to_x * 2 + side, first + x * 2 + core, device(0, side, to_x, dz),
-                           (batch, dx, c) == (1, 0, 0))
+                    yield (first + to_x * 2 + side, first + x * 2 + core, device(0, side, to_x, 0),
+                           (dx, c) == (0, 0))
 
     def home_legs(batch):
         first = FIRST[batch]
@@ -160,35 +162,70 @@
                     yield (first + to_x * 2 + side, first + x * 2 + core,
                            device(0, side, to_x, -(batch - 1) * sign), (batch, dx, c) == (1, 0, 0))
 
-    def send_out(batch):
-        for here, there, to, own in out_legs(batch):
+    def send_out(batch, parts=()):
+        for here, there, to, own in out_legs(batch, parts):
             if own:
                 pltpu.make_async_copy(tx.at[here], rx.at[there], recv_sem.at[batch]).start()
             else:
                 remote(tx.at[here], rx.at[there], send_sem.at[0], recv_sem.at[batch], to).start()
 
-    one_t, two_t = routes_t[0:1], routes_t[1:2]
     square = (rows, rows)
     down, across = lax.broadcasted_iota(jnp.int32, square, 0), lax.broadcasted_iota(jnp.int32, square, 1)
     early = (down < across).astype(F32).astype(BF16)
     late = (across < down).astype(F32).astype(BF16)
-    for batch in SEND_ORDER:
-        size = SIZES[batch]
-        line = lax.broadcasted_iota(jnp.int32, (size * cap, rows), 0)
-        expert = expert_of(line // cap, batch)
-        named = (one_t == expert) | (two_t == expert)
+    one_t, two_t = routes_t[0:1], routes_t[1:2]
+
+    def pack(count, move, to_x_of, slot_of, who):
+        if who == 0:
+            main, tan_rows, first, second = modded, modded_tan, one_t, two_t
+        else:
+            main, tan_rows = around.at[who - 1, 0], around.at[who - 1, 1]
+            first, second = routes_around[who - 1, 0:1], routes_around[who - 1, 1:2]
+        line = lax.broadcasted_iota(jnp.int32, (count * cap, rows), 0)
+        base = (0, -1, 1)[who]
+        expert = to_x_of(line // cap) * Z + (z + base + move(line // cap) + Z) % Z
+        named = (first == expert) | (second == expert)
         rank = jnp.dot(named.astype(F32).astype(BF16), early, preferred_element_type=F32)
         pick = (named & (rank == (line % cap).astype(F32))).astype(F32).astype(BF16)
 
         @pl.loop(0, width // 512)
-        def _(n, batch=batch, size=size, pick=pick):
+        def _(n):
             cols = pl.ds(pl.multiple_of(n * 512, 512), 512)
-            for source, first in ((modded, 0), (modded_tan, cap)):
+            for source, at in ((main, 0), (tan_rows, cap)):
                 packed = jnp.dot(pick, source[:, cols], preferred_element_type=F32).astype(BF16)
-                tx[pl.ds(FIRST[batch], size), pl.ds(first, cap), cols] = packed.reshape(size, cap, 512)
-
-        if batch not in HELD_BACK:
-            send_out(batch)
+                packed = packed.reshape(count, cap, 512)
+                for start, size, slot in slot_of:
+                    tx[pl.ds(slot, size), pl.ds(at, cap), cols] = packed[start:start + size]
+
+    around_copies = []
+    for side, dz in ((0, 1), (1, -1)):
+        to = device(0, core, x, dz)
+        for j, source in enumerate((modded, modded_tan)):
+            around_copies.append(
+                remote(source, around.at[side, j], around_send.at[0], around_recv.at[side], to))
+    for copy in around_copies:
+        copy.start()
+
+    pack(4, lambda b: 0 * b, lambda b: b, [(0, 4, 0)], 0)
+    send_out(0, (0,))
+    pack(8, lambda b: 2 - 4 * (b % 2), lambda b: b // 2, [(0, 8, FIRST[1])], 0)
+    send_out(1)
+
+    def pack_around():
+        for copy in route_copies:
+            copy.wait()
+        for side in range(2):
+            wait_bytes(around.at[side], around_recv.at[side])
+            up = 1 - 2 * side
+            odd = (x + side) % 2
+            pack(
+                10, lambda b: up * jnp.where(b < 4, 1, jnp.where(b < 8, 3, 4)),
+                lambda b: jnp.where(b < 8, b % X, 2 * (b - 8) + odd),
+                [(0, 4, 4 + 4 * side)] + [(4 + j, 1, FIRST[2] + 2 * j + side) for j in range(4)]
+                + [(8 + j, 1, FIRST[3] + 2 * j + odd) for j in range(2)], 1 + side)
+        send_out(0, (1, 2))
+        send_out(3)
+        send_out(2)
 
     turn = (((1,), (1,)), ((), ()))
     logits = lax.dot_general(modded[...], router[...], turn, preferred_element_type=F32)
@@ -309,9 +346,8 @@
                 near_copy(*units[u + WINDOW], kind).start()
         for kind in (UP, DOWN):
             spread_weights(a, k, kind)
-        if u == TOKENS_AT:
-            for batch in HELD_BACK:
-                send_out(batch)
+        if u == RELAY_AT:
+            pack_around()
         if u > 0:
             pass_weights(*units[u - 1])
         if u == EARLY:
@@ -347,7 +383,8 @@
                 out_tan[:, cols] = (
                     tan[:, cols].astype(F32) + gate_tan * mixture + gate * mixture_tan).astype(BF16)
 
-    wait_bytes(tx.at[pl.ds(0, SLOTS - 2)], send_sem.at[0])
+    wait_bytes(tx.at[pl.ds(0, SLOTS - 5)], send_sem.at[0])
+    wait_bytes(around, around_send.at[0])
     wait_bytes(rx.at[pl.ds(0, SLOTS - 2)], ret_send.at[0])
     for a in range(2):
         wait_bytes(held[a].at[0, pl.ds(0, 2 * part[a])], near_send.at[a])
@@ -384,6 +421,8 @@
         scratch_shapes=[
             pltpu.VMEM((rows, width), BF16),
             pltpu.VMEM((rows, width), BF16),
+            pltpu.VMEM((2, 2, rows, width), BF16),
+            pltpu.VMEM((2, 2, rows), jnp.int32),
             blocks, blocks, blocks,
             pltpu.VMEM((2 * rows, width), F32),
             mix, mix,
@@ -399,6 +438,7 @@
             *[pltpu.VMEM((1, width), F32)] * 2,
             dma((1,)), dma((len(SIZES),)), dma((1,)), dma((len(SIZES),)), dma((2,)),
             dma((2,)), dma((2, units)),
+            dma((3,)), dma((2,)), dma((2,)),
             dma((2, 2)), dma((2,)), dma((units, 2)), dma((2,)), dma((2, 2)), dma((2, 2)),
         ],
         compiler_params=pltpu.CompilerParams(

time: 212 us -> 206 us (0.972)
  the two profiles are of different devices: /device:TPU:1 before, /device:TPU:77 now
where the time goes in v4:
time: 206 us
  Pallas kernels  200 us (97%)
  local copies, waits for them, and re-layouts  4.13 us (2%)
    pallas_call x1, Pallas kernels, local(): pl.pallas_call(kernel, out_shape=(shape, shape), in_specs=[vmem, vmem, sm...  200 us
    unnamed x2, local copies, waits for them, and re-layouts  4.13 us

profile of v4, /device:TPU:77, one launch (start us, length us, event | category | flops | bytes accessed | tf_op | source)
XLA Modules:
  0.0 205.9 jit_solution(11375089182559253852)
XLA Ops:
  1.3 200.5 %shard_map.122 = (bf16[128,3072]{1,0:T(8,128)(2,1)}, bf16[128,3072]{1,0:T(8,128)(2,1)}) custom-call(bf16[128,3072]{1,0:T(8,128)(2,1)} %tok.1, bf16[128,3072]{1,0:T(8,128)(2,1)} %tan.1, s32[1]{0:T(128)S(6)} %copy.15.bucket, bf16[3,8,3072]{2,1,0:T(8,128)(2,1)} %bitcast.5, bf16[3,8,3072]{2,1,0:T(8,128)(2,1)} %bitcast.6, bf16[32,3072]{1,0:T(8,128)(2,1)} %bitcast.4, ...), custom_call_target="tpu_custom_call" | custom-call | tf_op jit(solution)/shard_map/pallas_call | solution.py:416
  201.8 2.1 %copy.16 = bf16[128,3072]{1,0:T(8,128)(2,1)} copy(bf16[128,3072]{1,0:T(8,128)(2,1)} %get-tuple-element.4) | data formatting | bytes 1572864
  203.8 2.1 %copy.17 = bf16[128,3072]{1,0:T(8,128)(2,1)} copy(bf16[128,3072]{1,0:T(8,128)(2,1)} %get-tuple-element.5) | data formatting | bytes 1572864

commit v5 on v4

--- a/solution.py
+++ b/solution.py
@@ -17,7 +17,7 @@
 SIZES = (12, 8, 8, 4)
 FIRST = (0, 12, 20, 28)
 SLOTS = 32
-WORK_ORDER = (1, 2, 3)
+WORK_ORDER = (3, 2, 1)
 CHUNKS = 2
 WINDOW = 2
 EARLY = 3

time: 206 us -> 202 us (0.981)
  the two profiles are of different devices: /device:TPU:77 before, /device:TPU:1 now
where the time goes in v5:
time: 202 us
  Pallas kernels  197 us (98%)
  local copies, waits for them, and re-layouts  4.13 us (2%)
    pallas_call x1, Pallas kernels, local(): pl.pallas_call(kernel, out_shape=(shape, shape), in_specs=[vmem, vmem, sm...  197 us
    unnamed x2, local copies, waits for them, and re-layouts  4.13 us

profile of v5, /device:TPU:1, one launch (start us, length us, event | category | flops | bytes accessed | tf_op | source)
XLA Modules:
  0.0 202.1 jit_solution(2753096309372940822)
XLA Ops:
  1.3 196.6 %shard_map.122 = (bf16[128,3072]{1,0:T(8,128)(2,1)}, bf16[128,3072]{1,0:T(8,128)(2,1)}) custom-call(bf16[128,3072]{1,0:T(8,128)(2,1)} %tok.1, bf16[128,3072]{1,0:T(8,128)(2,1)} %tan.1, s32[1]{0:T(128)S(6)} %copy.15.bucket, bf16[3,8,3072]{2,1,0:T(8,128)(2,1)} %bitcast.5, bf16[3,8,3072]{2,1,0:T(8,128)(2,1)} %bitcast.6, bf16[32,3072]{1,0:T(8,128)(2,1)} %bitcast.4, ...), custom_call_target="tpu_custom_call" | custom-call | tf_op jit(solution)/shard_map/pallas_call | solution.py:416
  197.9 2.1 %copy.16 = bf16[128,3072]{1,0:T(8,128)(2,1)} copy(bf16[128,3072]{1,0:T(8,128)(2,1)} %get-tuple-element.4) | data formatting | bytes 1572864
  200.0 2.1 %copy.17 = bf16[128,3072]{1,0:T(8,128)(2,1)} copy(bf16[128,3072]{1,0:T(8,128)(2,1)} %get-tuple-element.5) | data formatting | bytes 1572864
